TPU v7x, 512 devices: a whole 4x8x8 slice. The times are simulated.
512 devices in a mesh: rep: 32 (over x, y), fsdp: 16 (over z, core).
Axes of the slice: x: 4, y: 8, z: 8, core: 2. Of those that a mesh axis runs over, the one named last changes fastest.
Arguments:
- grads: bfloat16 [8, 576, 2048], P(None, 'fsdp')
- momentum: float32 [32, 576, 2048], P('rep', 'fsdp')
- owners: int32 [8], replicated, may hold values from 0 to 31, as said below
Outputs:
- update: bfloat16 [8, 576, 2048], P(None, 'fsdp')
- new_momentum: float32 [32, 576, 2048], P('rep', 'fsdp')
Inputs may be any that keep to these rules, and one draw needn't show every extreme that they name: The owners are distinct; owner 0 and the last replica group always appear.
All inputs are finite; a program needn't handle non-finite values.
Results may differ from a plain program's by a relative error of at most 0.001.
Values may be sent and summed in bfloat16 or wider, within the bound.
No kernel may reach another device: no remote copies, remote signals or barrier semaphores. Data moves between devices by JAX's collectives and lax.ppermute only.
A program may use at most 64 MiB of HBM per device.

v0:
```python
import math

import jax
import jax.numpy as jnp
from jax import lax
from jax.sharding import PartitionSpec as P

ROWS = 576
COLS = 2048
ITERS = 3


EPSILON = 1e-07
MOMENTUM_BETA = 0.95
QUINTIC_A = 3.4445
QUINTIC_B = -4.775
QUINTIC_C = 2.0315


def from_root(shard, axis, root):
    mine = lax.axis_index(axis) == root
    return lax.psum(jnp.where(mine, shard, jnp.zeros_like(shard)), axis)


def matmul(left, right):
    return jnp.dot(left, right, precision=lax.Precision.HIGHEST, preferred_element_type=jnp.float32)


def form_gram(column_block):
    partial_gram = matmul(column_block, column_block.T)
    gram_whole = lax.psum(partial_gram, "fsdp")
    return (gram_whole, gram_whole)


def form_poly(gram_whole):
    return QUINTIC_B * gram_whole + QUINTIC_C * matmul(gram_whole, gram_whole)


def column_orthogonal(steered):
    column_block = lax.all_to_all(steered, "fsdp", split_axis=1, concat_axis=0, tiled=True)
    square_total = lax.psum(jnp.sum(column_block * column_block), "fsdp")
    column_block = column_block / (jnp.sqrt(square_total) + EPSILON)
    for iteration in range(ITERS):
        gram_part, gram_whole = form_gram(column_block)
        polynomial = form_poly(gram_whole)
        column_block = QUINTIC_A * column_block + matmul(polynomial, column_block)
    return lax.all_to_all(column_block, "fsdp", split_axis=0, concat_axis=1, tiled=True)


def shards(grads, momentum, owners):
    factor = 0.2 * math.sqrt(max(ROWS, COLS))
    my_group = lax.axis_index("rep")
    matrix_count = owners.shape[0]
    positions = jnp.arange(matrix_count, dtype=jnp.int32)
    is_mine = owners == my_group
    owns_one = jnp.any(is_mine)
    chosen = jnp.sum(jnp.where(is_mine, positions, 0))
    gradient = lax.dynamic_index_in_dim(grads, chosen, 0, keepdims=False).astype(jnp.float32)
    held_state = momentum[0]
    renewed = jnp.where(owns_one, MOMENTUM_BETA * held_state + gradient, held_state)
    steered = gradient + MOMENTUM_BETA * renewed
    row_block = column_orthogonal(steered)
    scaled_rows = (factor * row_block).astype(jnp.bfloat16)
    delivered = [
        from_root(scaled_rows, "rep", owners[matrix_index]) for matrix_index in range(matrix_count)
    ]
    update = jnp.stack(delivered)
    return (update, renewed[None])


def solution(mesh):
    in_specs = (P(None, "fsdp", None), P("rep", "fsdp", None), P())
    out_specs = (P(None, "fsdp", None), P("rep", "fsdp", None))
    return jax.shard_map(shards, mesh=mesh, in_specs=in_specs, out_specs=out_specs, check_vma=False)
```

profile of v0, /device:TPU:16, one launch (start us, length us, event | category | flops | bytes accessed | tf_op | source)
XLA Modules:
  0.0 647.4 jit_solution(12812694040417416024)
XLA Ops:
  7.2 0.0 all-reduce.6.cloned.1.call-start
  7.2 1.3 fusion.27
  8.5 1.3 compare_reduce_fusion
  11.7 3.2 broadcast_select_fusion
  15.0 1.8 multiply_add_fusion
  16.8 22.6 %all_to_all.23 = f32[36,16,128]{2,0,1:T(8,128)S(1)} all-to-all(f32[36,16,128]{2,0,1:T(8,128)S(1)} %multiply_add_fusion), channel_id=1, replica_groups=mesh['rep'=32,'fsdp'=16] {'fsdp'}, dimensions={1} | all-to-all | bytes 589824 | tf_op jit(solution)/shard_map/all_to_all | solution.py:40
  39.4 0.7 multiply_reduce_fusion
  40.1 25.2 %psum.84 = f32[]{:T(128)} all-reduce(f32[]{:T(128)} %multiply_reduce_fusion), channel_id=1, replica_groups=mesh['rep'=32,'fsdp'=16] {'fsdp'}, use_global_device_ids=true, to_apply=%region_3.4 | all-reduce | flops 1 | bytes 8 | tf_op jit(solution)/shard_map/psum | solution.py:41
  66.1 2.4 fusion.35
  68.5 0.0 all-reduce.6.cloned.1.call-update
  68.6 0.0 all-reduce.8.cloned.1.call-start
  68.6 117.9 %all-reduce.6.cloned.1.call-done = f32[576,576]{1,0:T(8,128)} async-done(((f32[576,576]{1,0:T(8,128)}), f32[576,576]{1,0:T(8,128)}) %all-reduce.6.cloned.1.call-update) | async-done | bytes 1327120 | tf_op jit(solution)/shard_map/psum | solution.py:31
  186.5 6.2 fusion.36
  192.7 1.4 fusion.12
  194.2 2.4 fusion.37
  196.6 0.0 all-reduce.8.cloned.1.call-update
  196.6 0.2 all-reduce.10.cloned.1.call-start
  196.8 117.6 %all-reduce.8.cloned.1.call-done = f32[576,576]{1,0:T(8,128)} async-done(((f32[576,576]{1,0:T(8,128)}), f32[576,576]{1,0:T(8,128)}) %all-reduce.8.cloned.1.call-update) | async-done | bytes 1327120 | tf_op jit(solution)/shard_map/psum | solution.py:31
  314.4 6.2 fusion.38
  320.6 1.4 fusion.15
  322.0 2.4 fusion.39
  324.4 0.0 all-reduce.10.cloned.1.call-update
  324.5 117.8 %all-reduce.10.cloned.1.call-done = f32[576,576]{1,0:T(8,128)} async-done(((f32[576,576]{1,0:T(8,128)}), f32[576,576]{1,0:T(8,128)}) %all-reduce.10.cloned.1.call-update) | async-done | bytes 1327120 | tf_op jit(solution)/shard_map/psum | solution.py:31
  442.2 6.2 fusion.40
  448.4 1.7 fusion.18
  450.1 0.7 all_to_all.9
  450.8 4.6 all-to-all-start.1
  455.4 0.0 all-reduce.12.cloned.1.call-start
  455.5 0.7 fusion.34
  461.2 6.7 %all-to-all-done.1 = f32[16,36,128]{2,1,0:T(8,128)S(1)} async-done(((f32[16,36,128]{2,1,0:T(8,128)}), f32[16,36,128]{2,1,0:T(8,128)S(1)}, u32[]{:S(2)}, u32[]{:S(2)}) %all-to-all-start.1) | async-done | bytes 294944 | tf_op jit(solution)/shard_map/all_to_all | solution.py:47
  467.8 0.1 select_bitcast_fusion
  467.9 0.8 stack.34
  468.7 0.1 select_bitcast_fusion.1
  468.8 0.8 stack.33
  469.6 0.8 stack.32
  470.3 0.8 stack.31
  471.1 0.8 stack.30
  471.9 0.7 stack.29
  472.7 0.8 stack.28
  473.5 0.8 stack.27
  474.2 0.0 all-reduce.12.cloned.1.call-update
  474.2 160.1 %all-reduce.12.cloned.1.call-done = (bf16[1,36,2048]{2,1,0:T(8,128)(2,1)}, bf16[1,36,2048]{2,1,0:T(8,128)(2,1)}, bf16[1,36,2048]{2,1,0:T(8,128)(2,1)}, bf16[1,36...) async-done(((bf16[1,36,2048]{2,1,0:T(8,128)(2,1)}, ...) | async-done | bytes 1179664 | tf_op jit(solution)/shard_map/psum | solution.py:22
  634.4 1.0 constant_dynamic-update-slice_fusion.7
  635.4 0.9 constant_dynamic-update-slice_fusion.6
  636.3 0.9 constant_dynamic-update-slice_fusion.5
  637.2 0.9 constant_dynamic-update-slice_fusion.4
  638.2 0.9 constant_dynamic-update-slice_fusion.3
  639.2 1.7 copy.29
  (27 shorter events, 0.3 us)
Async XLA Ops:
  7.2 179.4 %all-reduce.6.cloned.1.call-start = ((), (), s32[]{:S(2)}) async-start(), calls=%async_computation.2 | async-start | bytes 2949120 | tf_op jit(solution)/shard_map/psum | solution.py:31
  68.6 245.8 %all-reduce.8.cloned.1.call-start = ((), (), s32[]{:S(2)}) async-start(), calls=%async_computation.3 | async-start | bytes 2949120 | tf_op jit(solution)/shard_map/psum | solution.py:31
  186.5 6.2 copy-start
  196.6 245.6 %all-reduce.10.cloned.1.call-start = ((), (), s32[]{:S(2)}) async-start(), calls=%async_computation.4 | async-start | bytes 2949120 | tf_op jit(solution)/shard_map/psum | solution.py:31
  314.4 6.2 copy-start.1
  442.2 6.2 copy-start.2
  448.4 7.1 %copy-start.6 = (s32[8]{0:T(128)S(1)}, s32[8]{0:T(128)}, u32[]{:S(2)}) copy-start(s32[8]{0:T(128)} %param.5) | copy-start | bytes 100
  450.8 17.0 %all-to-all-start.1 = ((f32[16,36,128]{2,1,0:T(8,128)}), f32[16,36,128]{2,1,0:T(8,128)S(1)}, u32[]{:S(2)}, u32[]{:S(2)}) async-start(f32[16,36,128]{2,1,0:T(8,128)} %all_to_all.9), calls=%async_computation.1 | async-start | bytes 655360 | tf_op jit(solution)/shard_map/all_to_all | solution.py:47
  455.4 178.9 %all-reduce.12.cloned.1.call-start = ((), (), s32[]{:S(2)}) async-start(), calls=%async_computation.5 | async-start | bytes 2621440 | tf_op jit(solution)/shard_map/psum | solution.py:22
  634.4 4.7 copy-start.5
  634.4 4.7 copy-start.4
  634.4 4.8 copy-start.3
Sparse Core Ops, SparseCore 0:
  68.7 117.8 all-reduce.5
  196.7 117.6 all-reduce.7
  324.6 117.6 all-reduce.9
  474.4 159.9 all-reduce.11
where the time goes:
time: 648 us; the launch traced here: 647 us
  waiting for transfers between devices  520 us (80%)
  blocking collectives  47.8 us (7%)
  matrix products  30.3 us (5%)
  between operations  21.6 us (3%)
  local copies, waits for them, and re-layouts  14.1 us (2%)
  other arithmetic  8.51 us (1%)
    psum x3, waiting for transfers between devices, form_gram(): gram_whole = lax.psum(partial_gram, 'fsdp')  353 us
    psum x1, waiting for transfers between devices, from_root(): return lax.psum(jnp.where(mine, shard, jnp.zeros_like(shard)), axis)  160 us
    dot_general x9, matrix products, matmul(): jnp.dot(left, right, precision=lax.Precision.HIGHEST, preferred_element_t...  30.3 us
    psum x1, blocking collectives, column_orthogonal(): square_total = lax.psum(jnp.sum(column_block * column_block), 'fsdp')  25.2 us
    all_to_all x1, blocking collectives, column_orthogonal(): lax.all_to_all(steered, 'fsdp', split_axis=1, concat_axis=0, tiled=True)  22.6 us
  transfers between devices with their start and end apart: 5, of which 5 were waited for; matrix products, arithmetic and copies ran while one was open for 0% of the time, Pallas kernels for 0%

commit v1 on v0

v1 whole, which is shorter than its diff:
```python
import math

import jax
import jax.numpy as jnp
from jax import lax
from jax.experimental import pallas as pl
from jax.experimental.pallas import tpu as pltpu
from jax.sharding import PartitionSpec as P

ROWS = 576
COLS = 2048
MATS = 8
ITERS = 3
N_FSDP = 16
OWN = ROWS // N_FSDP
PAD = 40
TALL = PAD * N_FSDP
NX, NY = 4, 8
N_REP = NX * NY
HALF = OWN // 2
CHUNK = 512

EPSILON = 1e-07
MOMENTUM_BETA = 0.95
QUINTIC_A = 3.4445
QUINTIC_B = -4.775
QUINTIC_C = 2.0315

f32, bf16 = jnp.float32, jnp.bfloat16


def split(value):
    high = value.astype(bf16)
    low = (value - high.astype(f32)).astype(bf16)
    return high, low


def product(left, right):
    lh, ll = left
    rh, rl = right
    small = jnp.dot(lh, rl, preferred_element_type=f32) + jnp.dot(ll, rh, preferred_element_type=f32)
    return small + jnp.dot(lh, rh, preferred_element_type=f32)


def product_nt(left, right):
    lh, ll = left
    rh, rl = right

    def dot(a, b):
        return lax.dot_general(a, b, (((1,), (1,)), ((), ())), preferred_element_type=f32)

    return (dot(lh, rl) + dot(ll, rh)) + dot(lh, rh)


def orthogonal_kernel(me_ref, s_ref, u_ref, high_ref, low_ref, gram_ref, rows_ref):
    step = pl.program_id(0)
    steps = pl.num_programs(0)
    high, low = split(s_ref[...])
    high_ref[step] = high
    low_ref[step] = low
    part = product_nt((high, low), (high, low))

    @pl.when(step == 0)
    def _():
        gram_ref[...] = part

    @pl.when(step > 0)
    def _():
        gram_ref[...] += part

    @pl.when(step == steps - 1)
    def _():
        row = lax.broadcasted_iota(jnp.int32, (TALL, TALL), 0)
        col = lax.broadcasted_iota(jnp.int32, (TALL, TALL), 1)
        diagonal = row == col
        gram = gram_ref[...]
        total = jnp.sum(jnp.where(diagonal, gram, 0.0), axis=(0, 1), keepdims=True)
        inverse = 1.0 / (jnp.sqrt(total) + EPSILON)
        start = pl.multiple_of(me_ref[0] * PAD, 8)
        mine = pl.ds(start, PAD)

        def poly(gram, square):
            return jnp.where(diagonal, QUINTIC_A, 0.0) + QUINTIC_B * gram + QUINTIC_C * square

        g0 = gram * inverse * inverse
        g0s = split(g0)
        q1 = poly(g0, product(g0s, g0s))
        q1s = split(q1)
        g1 = product(split(product(q1s, g0s)), q1s)
        g1s = split(g1)
        q2 = poly(g1, product(g1s, g1s))
        q2s = split(q2)
        rows_ref[...] = q2
        q2_mine = rows_ref[mine, :]
        g2_mine = product(split(product(split(q2_mine), g1s)), q2s)
        square = product(split(g2_mine), q2s)
        square = product(split(product(split(square), g1s)), q2s)
        own = lax.broadcasted_iota(jnp.int32, (PAD, TALL), 0) + start
        here = lax.broadcasted_iota(jnp.int32, (PAD, TALL), 1)
        q3_mine = jnp.where(own == here, QUINTIC_A, 0.0) + QUINTIC_B * g2_mine + QUINTIC_C * square
        mix = split(product(split(product(split(q3_mine), q2s)), q1s))
        factor = 0.2 * math.sqrt(max(ROWS, COLS))
        for part in range(COLS // CHUNK):
            update = product(mix, (high_ref[part], low_ref[part])) * inverse * factor
            for block in range(CHUNK // 128):
                lane = part * (CHUNK // 128) + block
                iy, left = lane // 2, lane % 2
                for half in range(2):
                    ix = left * 2 + half
                    piece = update[half * HALF : (half + 1) * HALF, block * 128 : (block + 1) * 128]
                    u_ref[ix * NY + iy] = piece.astype(bf16)


def orthogonal_rows(position, whole):
    return pl.pallas_call(
        orthogonal_kernel,
        grid=(COLS // CHUNK,),
        out_shape=jax.ShapeDtypeStruct((N_REP, HALF, 128), bf16),
        in_specs=[
            pl.BlockSpec(memory_space=pltpu.SMEM),
            pl.BlockSpec((TALL, CHUNK), lambda i: (0, i)),
        ],
        out_specs=pl.BlockSpec((N_REP, HALF, 128), lambda i: (0, 0, 0)),
        scratch_shapes=[
            pltpu.VMEM((COLS // CHUNK, TALL, CHUNK), bf16),
            pltpu.VMEM((COLS // CHUNK, TALL, CHUNK), bf16),
            pltpu.VMEM((TALL, TALL), f32),
            pltpu.VMEM((TALL, TALL), f32),
        ],
        compiler_params=pltpu.CompilerParams(vmem_limit_bytes=48 * 1024 * 1024),
    )(position, whole)


def assemble_kernel(my_y_ref, *refs):
    out_ref = refs[-1]
    for distance in range(NY):
        lane = lax.rem(my_y_ref[0] + NY - distance, NY) * 256
        for left in range(2):
            upper = refs[distance][2 * left].astype(f32)
            lower = refs[distance][2 * left + 1].astype(f32)
            lanes = pl.ds(pl.multiple_of(lane + left * 128, 128), 128)
            for mat in range(MATS):
                span = slice(mat * HALF, (mat + 1) * HALF)
                block = jnp.concatenate([upper[span], lower[span]], axis=0)
                out_ref[mat, :, lanes] = block.astype(bf16)


def assemble(my_y, parts):
    return pl.pallas_call(
        assemble_kernel,
        out_shape=jax.ShapeDtypeStruct((MATS, OWN, COLS), bf16),
        in_specs=[pl.BlockSpec(memory_space=pltpu.SMEM)] + [pl.BlockSpec(memory_space=pltpu.VMEM)] * NY,
        out_specs=pl.BlockSpec(memory_space=pltpu.VMEM),
        compiler_params=pltpu.CompilerParams(vmem_limit_bytes=32 * 1024 * 1024),
    )(my_y, *parts)


def shift_x(value, distance):
    pairs = [(x * NY + y, (x + distance) % NX * NY + y) for x in range(NX) for y in range(NY)]
    return lax.ppermute(value, "rep", pairs)


def shift_y(value, distance):
    pairs = [(x * NY + y, x * NY + (y + distance) % NY) for x in range(NX) for y in range(NY)]
    return lax.ppermute(value, "rep", pairs)


def deliver(pieces, owners):
    group = lax.axis_index("rep")
    my_x, my_y = group // NY, group % NY
    arrived = lax.all_to_all(pieces, "rep", split_axis=0, concat_axis=0, tiled=True)
    chosen = jnp.take(arrived, owners, axis=0, mode="clip").reshape(MATS * HALF, 128)
    along_x = [chosen] + [shift_x(chosen, d) for d in range(1, NX)]
    relative = jnp.stack(along_x[::-1] + along_x[:0:-1])
    absolute = lax.dynamic_slice_in_dim(relative, NX - 1 - my_x, NX, axis=0)
    along_y = [absolute] + [shift_y(absolute, d) for d in range(1, NY)]
    return assemble(my_y.astype(jnp.int32)[None], along_y)


def shards(grads, momentum, owners):
    my_group = lax.axis_index("rep")
    positions = jnp.arange(MATS, dtype=jnp.int32)
    is_mine = owners == my_group
    owns_one = jnp.any(is_mine)
    chosen = jnp.sum(jnp.where(is_mine, positions, 0))
    gradient = lax.dynamic_index_in_dim(grads, chosen, 0, keepdims=False).astype(f32)
    held_state = momentum[0]
    renewed = jnp.where(owns_one, MOMENTUM_BETA * held_state + gradient, held_state)
    steered = gradient + MOMENTUM_BETA * renewed
    padded = jnp.pad(steered, ((0, PAD - OWN), (0, 0)))
    whole = lax.all_gather(padded, "fsdp", axis=0, tiled=True)
    position = lax.axis_index("fsdp").astype(jnp.int32)[None]
    pieces = orthogonal_rows(position, whole)
    update = deliver(pieces, owners)
    return (update, renewed[None])


def solution(mesh):
    in_specs = (P(None, "fsdp", None), P("rep", "fsdp", None), P())
    out_specs = (P(None, "fsdp", None), P("rep", "fsdp", None))
    return jax.shard_map(shards, mesh=mesh, in_specs=in_specs, out_specs=out_specs, check_vma=False)
```

time: 648 us -> 176 us (0.27)
  the two profiles are of different devices: /device:TPU:16 before, /device:TPU:8 now
where the time goes in v1:
time: 176 us; the launch traced here: 175 us
  waiting for transfers between devices  79.7 us (45%)
  starting transfers between devices  44 us (25%)
  Pallas kernels  22.7 us (13%)
  between operations  16.2 us (9%)
  local copies, waits for them, and re-layouts  6.93 us (4%)
  other arithmetic  5.34 us (3%)
    all_gather x1, waiting for transfers between devices, shards(): whole = lax.all_gather(padded, 'fsdp', axis=0, tiled=True)  51.5 us
    ppermute x7, starting transfers between devices, shift_y(): return lax.ppermute(value, 'rep', pairs)  25.6 us
    pallas_call x1, Pallas kernels, orthogonal_rows(): pl.pallas_call(orthogonal_kernel, grid=(COLS // CHUNK,), out_shape=jax.Sh...  22.3 us
    ppermute x7, waiting for transfers between devices, shift_y(): return lax.ppermute(value, 'rep', pairs)  11.8 us
    all_to_all x1, waiting for transfers between devices, deliver(): lax.all_to_all(pieces, 'rep', split_axis=0, concat_axis=0, tiled=True)  11.4 us
    all_to_all x1, starting transfers between devices, deliver(): lax.all_to_all(pieces, 'rep', split_axis=0, concat_axis=0, tiled=True)  9.98 us
    ppermute x3, starting transfers between devices, shift_x(): return lax.ppermute(value, 'rep', pairs)  8.44 us
    unnamed x16, local copies, waits for them, and re-layouts  5.24 us
  transfers between devices with their start and end apart: 12, of which 7 were waited for; matrix products, arithmetic and copies ran while one was open for 1% of the time, Pallas kernels for 0%

profile of v1, /device:TPU:8, one launch (start us, length us, event | category | flops | bytes accessed | tf_op | source)
XLA Modules:
  0.0 174.9 jit_solution(13477650026549339685)
XLA Ops:
  7.2 0.0 copy-start
  7.2 0.0 all-gather.2.cloned.1.call-start
  7.2 1.4 fusion.5
  8.6 1.3 compare_reduce_fusion
  11.9 0.0 copy-done
  11.9 0.3 constant_dynamic-slice_fusion.1
  12.2 1.8 %fusion = f32[36,2048]{1,0:T(8,128)S(1)} fusion(f32[1,36,2048]{2,0,1:T(1,128)} %param.4, pred[]{:T(512)} %compare_reduce_fusion, bf16[1,36,2048]{2,0,1:T(2,128)(2,1)S(1)} %constant_dynamic-slice_fusion.1), kind=kLoop, calls=%fused_computation.3 | loop fusion | flops 442368 | bytes 737281 | tf_op jit(solution)/shard_map/add | solution.py:189
  14.0 0.8 pad.4
  14.8 0.0 all-gather.2.cloned.1.call-update
  14.8 51.5 %all-gather.2.cloned.1.call-done.s_ref = f32[640,2048]{1,0:T(8,128)} async-done(((f32[40,2048]{1,0:T(8,128)}), f32[640,2048]{1,0:T(8,128)}) %all-gather.2.cloned.1.call-update) | async-done | bytes 5242896 | tf_op jit(solution)/shard_map/all_gather | solution.py:191
  66.3 0.0 copy-start.1
  66.3 2.5 %copy-done.1 = f32[640,2048]{1,0:T(8,128)S(1)} copy-done((f32[640,2048]{1,0:T(8,128)S(1)}, f32[640,2048]{1,0:T(8,128)}, u32[]{:S(2)}) %copy-start.1) | copy-done | bytes 5242904
  68.8 0.0 copy-start.3
  68.8 22.3 %shard_map.50 = bf16[32,18,128]{2,1,0:T(8,128)(2,1)} custom-call(s32[1]{0:T(128)} %bitcast.1.me_ref, f32[640,2048]{1,0:T(8,128)S(1)} %copy-done.1), custom_call_target="tpu_custom_call" | custom-call | tf_op jit(solution)/shard_map/pallas_call | solution.py:115
  91.1 0.0 copy-start.2
  91.1 10.0 %all-to-all-start = ((bf16[32,18,128]{2,1,0:T(8,128)(2,1)}), bf16[32,18,128]{2,1,0:T(8,128)(2,1)S(1)}, u32[]{:S(2)}, u32[]{:S(2)}) async-start(bf16[32,18,128]{2,1,0:T(8,128)(2,1)} %shard_map.50), calls=%async_computation | async-start | bytes 393216 | tf_op jit(solution)/shard_map/all_to_all | solution.py:171
  101.1 0.0 copy-done.3
  101.1 11.4 %all-to-all-done = bf16[32,18,128]{2,1,0:T(8,128)(2,1)S(1)} async-done(((bf16[32,18,128]{2,1,0:T(8,128)(2,1)}), bf16[32,18,128]{2,1,0:T(8,128)(2,1)S(1)}, u32[]{:S(2)}, u32[]{:S(2)}) %all-to-all-start) | async-done | bytes 147488 | tf_op jit(solution)/shard_map/all_to_all | solution.py:171
  112.5 0.6 gather_fusion
  113.1 3.1 %collective-permute-start = (bf16[144,128]{1,0:T(8,128)(2,1)S(1)}, bf16[144,128]{1,0:T(8,128)(2,1)S(1)}, u32[]{:S(2)}, u32[]{:S(2)}) collective-permute-start(bf16[144,128]{1,0:T(8,128)(2,1)S(1)} %reshape.9), channel_id=1, source_target_pairs={{0,384},{16,400},{32,416},{48,432},{64,448},{80,464},{96,480},{112... | collective-permute-start | bytes 110600 | tf_op jit(solution)/shard_map/ppermute | solution.py:160
  116.2 3.4 %collective-permute-start.1 = (bf16[144,128]{1,0:T(8,128)(2,1)S(1)}, bf16[144,128]{1,0:T(8,128)(2,1)S(1)}, u32[]{:S(2)}, u32[]{:S(2)}) collective-permute-start(bf16[144,128]{1,0:T(8,128)(2,1)S(1)} %reshape.9), channel_id=1, source_target_pairs={{0,256},{16,272},{32,288},{48,304},{64,320},{80,336},{96,352},{112... | collective-permute-start | bytes 110600 | tf_op jit(solution)/shard_map/ppermute | solution.py:160
  119.6 2.0 %collective-permute-start.2 = (bf16[144,128]{1,0:T(8,128)(2,1)S(1)}, bf16[144,128]{1,0:T(8,128)(2,1)S(1)}, u32[]{:S(2)}, u32[]{:S(2)}) collective-permute-start(bf16[144,128]{1,0:T(8,128)(2,1)S(1)} %reshape.9), channel_id=1, source_target_pairs={{0,128},{16,144},{32,160},{48,176},{64,192},{80,208},{96,224},{112... | collective-permute-start | bytes 110600 | tf_op jit(solution)/shard_map/ppermute | solution.py:160
  121.6 0.0 collective-permute-done
  121.6 1.9 %collective-permute-done.1 = bf16[144,128]{1,0:T(8,128)(2,1)S(1)} collective-permute-done((bf16[144,128]{1,0:T(8,128)(2,1)S(1)}, bf16[144,128]{1,0:T(8,128)(2,1)S(1)}, u32[]{:S(2)}, u32[]{:S(2)}) %collective-permute-start.1) | collective-permute-done | bytes 36896 | tf_op jit(solution)/shard_map/ppermute | solution.py:160
  123.5 3.1 %collective-permute-done.2 = bf16[144,128]{1,0:T(8,128)(2,1)S(1)} collective-permute-done((bf16[144,128]{1,0:T(8,128)(2,1)S(1)}, bf16[144,128]{1,0:T(8,128)(2,1)S(1)}, u32[]{:S(2)}, u32[]{:S(2)}) %collective-permute-start.2) | collective-permute-done | bytes 36896 | tf_op jit(solution)/shard_map/ppermute | solution.py:160
  126.8 2.6 %collective-permute-start.3 = (bf16[4,144,128]{2,1,0:T(8,128)(2,1)S(1)}, bf16[4,144,128]{2,1,0:T(8,128)(2,1)S(1)}, u32[]{:S(2)}, u32[]{:S(2)}) collective-permute-start(bf16[4,144,128]{2,1,0:T(8,128)(2,1)S(1)} %constant_dynamic-slice_fusion.refs_0_), channel_id=1, source_target_pairs={{0,16},{16,32},{32,48},{48,64},{64,80},{80,96},{96,112},{112,0},{1... | collective-permute-start | bytes 442376 | tf_op jit(solution)/shard_map/ppermute | solution.py:165
  129.4 2.5 %collective-permute-start.4 = (bf16[4,144,128]{2,1,0:T(8,128)(2,1)S(1)}, bf16[4,144,128]{2,1,0:T(8,128)(2,1)S(1)}, u32[]{:S(2)}, u32[]{:S(2)}) collective-permute-start(bf16[4,144,128]{2,1,0:T(8,128)(2,1)S(1)} %constant_dynamic-slice_fusion.refs_0_), channel_id=1, source_target_pairs={{0,32},{16,48},{32,64},{48,80},{64,96},{80,112},{96,0},{112,16},{1... | collective-permute-start | bytes 442376 | tf_op jit(solution)/shard_map/ppermute | solution.py:165
  131.9 3.7 %collective-permute-start.5 = (bf16[4,144,128]{2,1,0:T(8,128)(2,1)S(1)}, bf16[4,144,128]{2,1,0:T(8,128)(2,1)S(1)}, u32[]{:S(2)}, u32[]{:S(2)}) collective-permute-start(bf16[4,144,128]{2,1,0:T(8,128)(2,1)S(1)} %constant_dynamic-slice_fusion.refs_0_), channel_id=1, source_target_pairs={{0,48},{16,64},{32,80},{48,96},{64,112},{80,0},{96,16},{112,32},{1... | collective-permute-start | bytes 442376 | tf_op jit(solution)/shard_map/ppermute | solution.py:165
  135.6 6.1 %collective-permute-start.6 = (bf16[4,144,128]{2,1,0:T(8,128)(2,1)S(1)}, bf16[4,144,128]{2,1,0:T(8,128)(2,1)S(1)}, u32[]{:S(2)}, u32[]{:S(2)}) collective-permute-start(bf16[4,144,128]{2,1,0:T(8,128)(2,1)S(1)} %constant_dynamic-slice_fusion.refs_0_), channel_id=1, source_target_pairs={{0,64},{16,80},{32,96},{48,112},{64,0},{80,16},{96,32},{112,48},{1... | collective-permute-start | bytes 442376 | tf_op jit(solution)/shard_map/ppermute | solution.py:165
  141.7 5.3 %collective-permute-start.7 = (bf16[4,144,128]{2,1,0:T(8,128)(2,1)S(1)}, bf16[4,144,128]{2,1,0:T(8,128)(2,1)S(1)}, u32[]{:S(2)}, u32[]{:S(2)}) collective-permute-start(bf16[4,144,128]{2,1,0:T(8,128)(2,1)S(1)} %constant_dynamic-slice_fusion.refs_0_), channel_id=1, source_target_pairs={{0,80},{16,96},{32,112},{48,0},{64,16},{80,32},{96,48},{112,64},{1... | collective-permute-start | bytes 442376 | tf_op jit(solution)/shard_map/ppermute | solution.py:165
  147.1 0.0 collective-permute-done.3.refs_1_
  147.1 2.2 %collective-permute-start.8 = (bf16[4,144,128]{2,1,0:T(8,128)(2,1)S(1)}, bf16[4,144,128]{2,1,0:T(8,128)(2,1)S(1)}, u32[]{:S(2)}, u32[]{:S(2)}) collective-permute-start(bf16[4,144,128]{2,1,0:T(8,128)(2,1)S(1)} %constant_dynamic-slice_fusion.refs_0_), channel_id=1, source_target_pairs={{0,96},{16,112},{32,0},{48,16},{64,32},{80,48},{96,64},{112,80},{1... | collective-permute-start | bytes 442376 | tf_op jit(solution)/shard_map/ppermute | solution.py:165
  149.3 0.0 collective-permute-done.4.refs_2_
  149.3 3.1 %collective-permute-start.9 = (bf16[4,144,128]{2,1,0:T(8,128)(2,1)S(1)}, bf16[4,144,128]{2,1,0:T(8,128)(2,1)S(1)}, u32[]{:S(2)}, u32[]{:S(2)}) collective-permute-start(bf16[4,144,128]{2,1,0:T(8,128)(2,1)S(1)} %constant_dynamic-slice_fusion.refs_0_), channel_id=1, source_target_pairs={{0,112},{16,0},{32,16},{48,32},{64,48},{80,64},{96,80},{112,96},{1... | collective-permute-start | bytes 442376 | tf_op jit(solution)/shard_map/ppermute | solution.py:165
  152.4 0.0 copy-done.2
  152.4 0.8 fusion.4
  153.2 1.0 copy.14
  154.3 0.0 collective-permute-done.5.refs_3_
  154.3 0.0 collective-permute-done.6.refs_4_
  154.3 6.8 %collective-permute-done.7.refs_5_ = bf16[4,144,128]{2,1,0:T(8,128)(2,1)S(1)} collective-permute-done((bf16[4,144,128]{2,1,0:T(8,128)(2,1)S(1)}, bf16[4,144,128]{2,1,0:T(8,128)(2,1)S(1)}, u32[]{:S(2)}, u32[]{:S(2)}) %collective-permute-start.7) | collective-permute-done | bytes 147488 | tf_op jit(solution)/shard_map/ppermute | solution.py:165
  161.1 2.9 %collective-permute-done.8.refs_6_ = bf16[4,144,128]{2,1,0:T(8,128)(2,1)S(1)} collective-permute-done((bf16[4,144,128]{2,1,0:T(8,128)(2,1)S(1)}, bf16[4,144,128]{2,1,0:T(8,128)(2,1)S(1)}, u32[]{:S(2)}, u32[]{:S(2)}) %collective-permute-start.8) | collective-permute-done | bytes 147488 | tf_op jit(solution)/shard_map/ppermute | solution.py:165
  164.0 2.0 %collective-permute-done.9.refs_7_ = bf16[4,144,128]{2,1,0:T(8,128)(2,1)S(1)} collective-permute-done((bf16[4,144,128]{2,1,0:T(8,128)(2,1)S(1)}, bf16[4,144,128]{2,1,0:T(8,128)(2,1)S(1)}, u32[]{:S(2)}, u32[]{:S(2)}) %collective-permute-start.9) | collective-permute-done | bytes 147488 | tf_op jit(solution)/shard_map/ppermute | solution.py:165
  166.0 0.4 shard_map.51
  166.4 1.7 copy.13
  (11 shorter events, 0.1 us)
Async XLA Ops:
  7.2 4.7 %copy-start = (bf16[8,36,2048]{2,0,1:T(8,128)(2,1)S(1)}, bf16[8,36,2048]{2,0,1:T(8,128)(2,1)}, u32[]{:S(2)}) copy-start(bf16[8,36,2048]{2,0,1:T(8,128)(2,1)} %param.3) | copy-start | bytes 3538948
  7.2 59.1 %all-gather.2.cloned.1.call-start = ((), (), s32[]{:S(2)}) async-start(), calls=%async_computation.1 | async-start | bytes 5570560 | tf_op jit(solution)/shard_map/all_gather | solution.py:191
  66.3 2.5 %copy-start.1 = (f32[640,2048]{1,0:T(8,128)S(1)}, f32[640,2048]{1,0:T(8,128)}, u32[]{:S(2)}) copy-start(f32[640,2048]{1,0:T(8,128)} %all-gather.2.cloned.1.call-done.s_ref) | copy-start | bytes 15728644
  68.8 32.3 %copy-start.3 = (s32[8]{0:T(128)S(1)}, s32[8]{0:T(128)}, u32[]{:S(2)}) copy-start(s32[8]{0:T(128)} %param.5) | copy-start | bytes 100
  91.1 61.3 %copy-start.2 = (f32[1,36,2048]{2,0,1:T(1,128)S(1)}, f32[1,36,2048]{2,0,1:T(1,128)}, u32[]{:S(2)}) copy-start(f32[1,36,2048]{2,0,1:T(1,128)} %param.4) | copy-start | bytes 884740
  91.1 21.4 %all-to-all-start = ((bf16[32,18,128]{2,1,0:T(8,128)(2,1)}), bf16[32,18,128]{2,1,0:T(8,128)(2,1)S(1)}, u32[]{:S(2)}, u32[]{:S(2)}) async-start(bf16[32,18,128]{2,1,0:T(8,128)(2,1)} %shard_map.50), calls=%async_computation | async-start | bytes 393216 | tf_op jit(solution)/shard_map/all_to_all | solution.py:171
  113.1 8.5 %collective-permute-start = (bf16[144,128]{1,0:T(8,128)(2,1)S(1)}, bf16[144,128]{1,0:T(8,128)(2,1)S(1)}, u32[]{:S(2)}, u32[]{:S(2)}) collective-permute-start(bf16[144,128]{1,0:T(8,128)(2,1)S(1)} %reshape.9), channel_id=1, source_target_pairs={{0,384},{16,400},{32,416},{48,432},{64,448},{80,464},{96,480},{112... | collective-permute-start | bytes 110600 | tf_op jit(solution)/shard_map/ppermute | solution.py:160
  116.2 7.4 %collective-permute-start.1 = (bf16[144,128]{1,0:T(8,128)(2,1)S(1)}, bf16[144,128]{1,0:T(8,128)(2,1)S(1)}, u32[]{:S(2)}, u32[]{:S(2)}) collective-permute-start(bf16[144,128]{1,0:T(8,128)(2,1)S(1)} %reshape.9), channel_id=1, source_target_pairs={{0,256},{16,272},{32,288},{48,304},{64,320},{80,336},{96,352},{112... | collective-permute-start | bytes 110600 | tf_op jit(solution)/shard_map/ppermute | solution.py:160
  119.6 7.1 %collective-permute-start.2 = (bf16[144,128]{1,0:T(8,128)(2,1)S(1)}, bf16[144,128]{1,0:T(8,128)(2,1)S(1)}, u32[]{:S(2)}, u32[]{:S(2)}) collective-permute-start(bf16[144,128]{1,0:T(8,128)(2,1)S(1)} %reshape.9), channel_id=1, source_target_pairs={{0,128},{16,144},{32,160},{48,176},{64,192},{80,208},{96,224},{112... | collective-permute-start | bytes 110600 | tf_op jit(solution)/shard_map/ppermute | solution.py:160
  126.8 20.3 %collective-permute-start.3 = (bf16[4,144,128]{2,1,0:T(8,128)(2,1)S(1)}, bf16[4,144,128]{2,1,0:T(8,128)(2,1)S(1)}, u32[]{:S(2)}, u32[]{:S(2)}) collective-permute-start(bf16[4,144,128]{2,1,0:T(8,128)(2,1)S(1)} %constant_dynamic-slice_fusion.refs_0_), channel_id=1, source_target_pairs={{0,16},{16,32},{32,48},{48,64},{64,80},{80,96},{96,112},{112,0},{1... | collective-permute-start | bytes 442376 | tf_op jit(solution)/shard_map/ppermute | solution.py:165
  129.4 19.9 %collective-permute-start.4 = (bf16[4,144,128]{2,1,0:T(8,128)(2,1)S(1)}, bf16[4,144,128]{2,1,0:T(8,128)(2,1)S(1)}, u32[]{:S(2)}, u32[]{:S(2)}) collective-permute-start(bf16[4,144,128]{2,1,0:T(8,128)(2,1)S(1)} %constant_dynamic-slice_fusion.refs_0_), channel_id=1, source_target_pairs={{0,32},{16,48},{32,64},{48,80},{64,96},{80,112},{96,0},{112,16},{1... | collective-permute-start | bytes 442376 | tf_op jit(solution)/shard_map/ppermute | solution.py:165
  131.9 22.4 %collective-permute-start.5 = (bf16[4,144,128]{2,1,0:T(8,128)(2,1)S(1)}, bf16[4,144,128]{2,1,0:T(8,128)(2,1)S(1)}, u32[]{:S(2)}, u32[]{:S(2)}) collective-permute-start(bf16[4,144,128]{2,1,0:T(8,128)(2,1)S(1)} %constant_dynamic-slice_fusion.refs_0_), channel_id=1, source_target_pairs={{0,48},{16,64},{32,80},{48,96},{64,112},{80,0},{96,16},{112,32},{1... | collective-permute-start | bytes 442376 | tf_op jit(solution)/shard_map/ppermute | solution.py:165
  135.6 18.7 %collective-permute-start.6 = (bf16[4,144,128]{2,1,0:T(8,128)(2,1)S(1)}, bf16[4,144,128]{2,1,0:T(8,128)(2,1)S(1)}, u32[]{:S(2)}, u32[]{:S(2)}) collective-permute-start(bf16[4,144,128]{2,1,0:T(8,128)(2,1)S(1)} %constant_dynamic-slice_fusion.refs_0_), channel_id=1, source_target_pairs={{0,64},{16,80},{32,96},{48,112},{64,0},{80,16},{96,32},{112,48},{1... | collective-permute-start | bytes 442376 | tf_op jit(solution)/shard_map/ppermute | solution.py:165
  141.7 19.4 %collective-permute-start.7 = (bf16[4,144,128]{2,1,0:T(8,128)(2,1)S(1)}, bf16[4,144,128]{2,1,0:T(8,128)(2,1)S(1)}, u32[]{:S(2)}, u32[]{:S(2)}) collective-permute-start(bf16[4,144,128]{2,1,0:T(8,128)(2,1)S(1)} %constant_dynamic-slice_fusion.refs_0_), channel_id=1, source_target_pairs={{0,80},{16,96},{32,112},{48,0},{64,16},{80,32},{96,48},{112,64},{1... | collective-permute-start | bytes 442376 | tf_op jit(solution)/shard_map/ppermute | solution.py:165
  147.1 16.9 %collective-permute-start.8 = (bf16[4,144,128]{2,1,0:T(8,128)(2,1)S(1)}, bf16[4,144,128]{2,1,0:T(8,128)(2,1)S(1)}, u32[]{:S(2)}, u32[]{:S(2)}) collective-permute-start(bf16[4,144,128]{2,1,0:T(8,128)(2,1)S(1)} %constant_dynamic-slice_fusion.refs_0_), channel_id=1, source_target_pairs={{0,96},{16,112},{32,0},{48,16},{64,32},{80,48},{96,64},{112,80},{1... | collective-permute-start | bytes 442376 | tf_op jit(solution)/shard_map/ppermute | solution.py:165
  149.3 16.7 %collective-permute-start.9 = (bf16[4,144,128]{2,1,0:T(8,128)(2,1)S(1)}, bf16[4,144,128]{2,1,0:T(8,128)(2,1)S(1)}, u32[]{:S(2)}, u32[]{:S(2)}) collective-permute-start(bf16[4,144,128]{2,1,0:T(8,128)(2,1)S(1)} %constant_dynamic-slice_fusion.refs_0_), channel_id=1, source_target_pairs={{0,112},{16,0},{32,16},{48,32},{64,48},{80,64},{96,80},{112,96},{1... | collective-permute-start | bytes 442376 | tf_op jit(solution)/shard_map/ppermute | solution.py:165
Sparse Core Ops, SparseCore 0:
  14.9 51.3 all-gather.1

commit v2 on v0

v2 whole, which is shorter than its diff:
```python
import math

import jax
import jax.numpy as jnp
from jax import lax
from jax.experimental import pallas as pl
from jax.experimental.pallas import tpu as pltpu
from jax.sharding import PartitionSpec as P

ROWS = 576
COLS = 2048
MATS = 8
ITERS = 3
N_FSDP = 16
OWN = ROWS // N_FSDP
PAD = 40
TALL = PAD * N_FSDP
NX, NY = 4, 8
N_REP = NX * NY
HALF = OWN // 2
CHUNK = 512

EPSILON = 1e-07
MOMENTUM_BETA = 0.95
QUINTIC_A = 3.4445
QUINTIC_B = -4.775
QUINTIC_C = 2.0315

f32, bf16 = jnp.float32, jnp.bfloat16


def split(value):
    high = value.astype(bf16)
    low = (value - high.astype(f32)).astype(bf16)
    return high, low


def dot(left, right):
    return jnp.dot(left, right, preferred_element_type=f32)


def dot_nt(left, right):
    return lax.dot_general(left, right, (((1,), (1,)), ((), ())), preferred_element_type=f32)


def product(left, right):
    (lh, ll), (rh, rl) = left, right
    return (dot(lh, rl) + dot(ll, rh)) + dot(lh, rh)


def square(halves):
    high, low = halves
    cross = dot(high, low)
    return (cross + cross.T) + dot(high, high)


def thin_product(rows, halves):
    high, low = halves
    kept = rows.astype(bf16).astype(f32)
    stacked = jnp.concatenate([kept, rows - kept], axis=0).astype(bf16)
    first = dot(stacked, high)
    second = dot(stacked, low)
    return first[:PAD] + (first[PAD:] + second[:PAD])


def orthogonal_kernel(me_ref, s_hbm, u_ref, s_ref, high_ref, low_ref, rows_ref, sems):
    chunks = COLS // CHUNK

    def fetch(part):
        lanes = pl.ds(part * CHUNK, CHUNK)
        return pltpu.make_async_copy(s_hbm.at[:, lanes], s_ref.at[part], sems.at[part])

    for part in range(chunks):
        fetch(part).start()
    gram = None
    cross = None
    for part in range(chunks):
        fetch(part).wait()
        high, low = split(s_ref[part])
        high_ref[part] = high
        low_ref[part] = low
        more_cross, more = dot_nt(high, low), dot_nt(high, high)
        cross = more_cross if part == 0 else cross + more_cross
        gram = more if part == 0 else gram + more
    gram = gram + (cross + cross.T)

    row = lax.broadcasted_iota(jnp.int32, (TALL, TALL), 0)
    col = lax.broadcasted_iota(jnp.int32, (TALL, TALL), 1)
    diagonal = row == col
    total = jnp.sum(jnp.where(diagonal, gram, 0.0), axis=(0, 1), keepdims=True)
    inverse = 1.0 / (jnp.sqrt(total) + EPSILON)
    start = pl.multiple_of(me_ref[0] * PAD, 8)

    def poly(gram, squared):
        return jnp.where(diagonal, QUINTIC_A, 0.0) + QUINTIC_B * gram + QUINTIC_C * squared

    g0 = gram * inverse * inverse
    g0s = split(g0)
    q1s = split(poly(g0, square(g0s)))
    g1 = product(g0s, split(square(q1s)))
    g1s = split(g1)
    q2 = poly(g1, square(g1s))
    q2s = split(q2)
    rows_ref[...] = q2
    mixed = thin_product(rows_ref[pl.ds(start, PAD), :], q1s)

    def by_g2(rows):
        return thin_product(thin_product(thin_product(rows, g1s), q2s), q2s)

    once = by_g2(mixed)
    twice = by_g2(once)
    mixed = QUINTIC_A * mixed + QUINTIC_B * once + QUINTIC_C * twice
    factor = 0.2 * math.sqrt(max(ROWS, COLS))
    for part in range(chunks):
        update = thin_product(mixed, (high_ref[part], low_ref[part])) * inverse * factor
        for block in range(CHUNK // 128):
            lane = part * (CHUNK // 128) + block
            iy, left = lane // 2, lane % 2
            for half in range(2):
                ix = left * 2 + half
                piece = update[half * HALF : (half + 1) * HALF, block * 128 : (block + 1) * 128]
                u_ref[ix * NY + iy] = piece.astype(bf16)


def orthogonal_rows(position, whole):
    chunks = COLS // CHUNK
    return pl.pallas_call(
        orthogonal_kernel,
        out_shape=jax.ShapeDtypeStruct((N_REP, HALF, 128), bf16),
        in_specs=[
            pl.BlockSpec(memory_space=pltpu.SMEM),
            pl.BlockSpec(memory_space=pltpu.HBM),
        ],
        out_specs=pl.BlockSpec(memory_space=pltpu.VMEM),
        scratch_shapes=[
            pltpu.VMEM((chunks, TALL, CHUNK), f32),
            pltpu.VMEM((chunks, TALL, CHUNK), bf16),
            pltpu.VMEM((chunks, TALL, CHUNK), bf16),
            pltpu.VMEM((TALL, TALL), f32),
            pltpu.SemaphoreType.DMA((chunks,)),
        ],
        compiler_params=pltpu.CompilerParams(vmem_limit_bytes=48 * 1024 * 1024),
    )(position, whole)


def choose_kernel(owners_ref, arrived_ref, out_ref, rows_ref):
    for mat in range(MATS):
        rows_ref[pl.ds(mat, HALF, stride=MATS), :] = arrived_ref[owners_ref[mat]].astype(f32)
    rows = rows_ref[...].astype(bf16)
    for copy in range(NY):
        out_ref[copy] = rows


def choose(owners, arrived):
    return pl.pallas_call(
        choose_kernel,
        out_shape=jax.ShapeDtypeStruct((NY, HALF * MATS, 128), bf16),
        in_specs=[pl.BlockSpec(memory_space=pltpu.SMEM), pl.BlockSpec(memory_space=pltpu.VMEM)],
        out_specs=pl.BlockSpec(memory_space=pltpu.VMEM),
        scratch_shapes=[pltpu.VMEM((HALF * MATS, 128), f32)],
        compiler_params=pltpu.CompilerParams(vmem_limit_bytes=16 * 1024 * 1024),
    )(owners, arrived)


def assemble_kernel(parts_ref, out_hbm, rows_ref, sems):
    def store(half):
        rows = pl.ds(half * HALF, HALF)
        return pltpu.make_async_copy(rows_ref.at[rows], out_hbm.at[rows], sems.at[half])

    for half in range(2):
        for iy in range(NY):
            for left in range(2):
                lane = (iy * 2 + left) * 128
                piece = parts_ref[2 * left + half, iy * HALF : (iy + 1) * HALF]
                rows_ref[half * HALF : (half + 1) * HALF, :, lane : lane + 128] = piece
        store(half).start()
    for half in range(2):
        store(half).wait()


def assemble(parts):
    return pl.pallas_call(
        assemble_kernel,
        out_shape=pltpu.HBM((OWN, MATS, COLS), bf16),
        in_specs=[pl.BlockSpec(memory_space=pltpu.VMEM)],
        out_specs=pl.BlockSpec(memory_space=pltpu.HBM),
        scratch_shapes=[pltpu.VMEM((OWN, MATS, COLS), bf16), pltpu.SemaphoreType.DMA((2,))],
        compiler_params=pltpu.CompilerParams(vmem_limit_bytes=32 * 1024 * 1024),
    )(parts)


def steer_kernel(
    group_ref, owners_hbm, grads_hbm, momentum_hbm, renewed_ref, steered_ref,
    owners_ref, grads_ref, momentum_ref, wide_ref, sems,
):
    blocks = COLS // 128
    chunks = COLS // CHUNK

    def fetch(part):
        lanes = pl.ds(part * CHUNK, CHUNK)
        return pltpu.make_async_copy(grads_hbm.at[:, :, lanes], grads_ref.at[part], sems.at[part])

    fetch_owners = pltpu.make_async_copy(owners_hbm, owners_ref, sems.at[chunks])
    fetch_momentum = pltpu.make_async_copy(momentum_hbm, momentum_ref, sems.at[chunks + 1])
    fetch_owners.start()
    fetch_momentum.start()
    for part in range(chunks):
        fetch(part).start()
    steered_ref[OWN:, :] = jnp.zeros((PAD - OWN, COLS), f32)
    fetch_owners.wait()
    owns_one = owners_ref[0] == group_ref[0]
    chosen = 0
    for index in range(1, MATS):
        here = owners_ref[index] == group_ref[0]
        owns_one = jnp.logical_or(owns_one, here)
        chosen = chosen + jnp.where(here, index, 0)
    fetch_momentum.wait()
    for block in range(blocks):
        part, inner = block // (CHUNK // 128), block % (CHUNK // 128)
        if inner == 0:
            fetch(part).wait()
        wide = grads_ref[part, :, :, inner * 128 : (inner + 1) * 128].astype(f32)
        wide_ref[block] = wide.reshape(OWN * MATS, 128)
        gradient = wide_ref[block, pl.ds(chosen, OWN, stride=MATS), :]
        held_state = momentum_ref[pl.ds(block, OWN, stride=blocks), :]
        renewed = jnp.where(owns_one, MOMENTUM_BETA * held_state + gradient, held_state)
        renewed_ref[pl.ds(block, OWN, stride=blocks), :] = renewed
        steered_ref[:OWN, block * 128 : (block + 1) * 128] = gradient + MOMENTUM_BETA * renewed


def in_hbm(value):
    return pltpu.with_memory_space_constraint(value, pltpu.HBM)


def steer(owners, group, grads, momentum):
    chunks = COLS // CHUNK
    return pl.pallas_call(
        steer_kernel,
        in_specs=[pl.BlockSpec(memory_space=pltpu.SMEM)] + [pl.BlockSpec(memory_space=pltpu.HBM)] * 3,
        out_specs=[pl.BlockSpec(memory_space=pltpu.VMEM)] * 2,
        out_shape=[
            jax.ShapeDtypeStruct((OWN * COLS // 128, 128), f32),
            jax.ShapeDtypeStruct((PAD, COLS), f32),
        ],
        scratch_shapes=[
            pltpu.SMEM((MATS,), jnp.int32),
            pltpu.VMEM((chunks, OWN, MATS, CHUNK), bf16),
            pltpu.VMEM((OWN * COLS // 128, 128), f32),
            pltpu.VMEM((COLS // 128, OWN * MATS, 128), f32),
            pltpu.SemaphoreType.DMA((chunks + 2,)),
        ],
        compiler_params=pltpu.CompilerParams(vmem_limit_bytes=32 * 1024 * 1024),
    )(group, in_hbm(owners), in_hbm(grads), in_hbm(momentum))


def exchange(copies, groups):
    return lax.all_to_all(copies, "rep", split_axis=0, concat_axis=0, tiled=True, axis_index_groups=groups)


def deliver(pieces, owners):
    along_y = [[x * NY + y for y in range(NY)] for x in range(NX)]
    along_x = [[x * NY + y for x in range(NX)] for y in range(NY)]
    arrived = lax.all_to_all(pieces, "rep", split_axis=0, concat_axis=0, tiled=True)
    column = exchange(choose(owners, arrived), along_y)
    copies = jnp.broadcast_to(column[None], (NX, *column.shape))
    parts = exchange(copies, along_x)
    rows = assemble(parts.reshape(NX, NY * HALF, MATS, 128))
    return rows.transpose(1, 0, 2)


def shards(grads, momentum, owners):
    group = lax.axis_index("rep").astype(jnp.int32)[None]
    position = lax.axis_index("fsdp").astype(jnp.int32)[None]
    flat = momentum.reshape(OWN * COLS // 128, 128)
    renewed, steered = steer(owners, group, grads.transpose(1, 0, 2), flat)
    whole = lax.all_gather(steered, "fsdp", axis=0, tiled=True)
    pieces = orthogonal_rows(position, in_hbm(whole))
    update = deliver(pieces, owners)
    return (update, renewed.reshape(1, OWN, COLS))


def solution(mesh):
    in_specs = (P(None, "fsdp", None), P("rep", "fsdp", None), P())
    out_specs = (P(None, "fsdp", None), P("rep", "fsdp", None))
    return jax.shard_map(shards, mesh=mesh, in_specs=in_specs, out_specs=out_specs, check_vma=False)
```

time: 648 us -> 140 us (0.22)
  the two profiles are of different devices: /device:TPU:16 before, /device:TPU:2 now
where the time goes in v2:
time: 140 us
  waiting for transfers between devices  52.6 us (38%)
  blocking collectives  51.6 us (37%)
  Pallas kernels  21.4 us (15%)
  between operations  14.1 us (10%)
    all_gather x1, waiting for transfers between devices, shards(): whole = lax.all_gather(steered, 'fsdp', axis=0, tiled=True)  52.5 us
    all_to_all x2, blocking collectives, exchange(): lax.all_to_all(copies, 'rep', split_axis=0, concat_axis=0, tiled=True, ax...  31.3 us
    all_to_all x1, blocking collectives, deliver(): lax.all_to_all(pieces, 'rep', split_axis=0, concat_axis=0, tiled=True)  20.3 us
    pallas_call x1, Pallas kernels, orthogonal_rows(): pl.pallas_call(orthogonal_kernel, out_shape=jax.ShapeDtypeStruct((N_REP,...  17.3 us
  transfers between devices with their start and end apart: 1, of which 1 were waited for; matrix products, arithmetic and copies ran while one was open for 0% of the time, Pallas kernels for 0%

profile of v2, /device:TPU:2, one launch (start us, length us, event | category | flops | bytes accessed | tf_op | source)
XLA Modules:
  0.0 139.8 jit_solution(1428446251962515185)
XLA Ops:
  7.2 0.0 all-gather.2.cloned.1.call-start
  7.2 2.4 %shard_map.50 = (f32[576,128]{1,0:T(8,128)}, f32[40,2048]{1,0:T(8,128)}) custom-call(s32[1]{0:T(128)} %bitcast.1.group_ref, s32[8]{0:T(128)} %owners_ref.1, bf16[36,8,2048]{2,1,0:T(8,128)(2,1)} %bitcast.8, f32[576,128]{1,0:T(8,128)} %bitcast.10), custom_call_target="tpu_custom_call" | custom-call | tf_op jit(solution)/shard_map/pallas_call | solution.py:237
  9.6 0.0 all-gather.2.cloned.1.call-update
  9.6 52.5 %all-gather.2.cloned.1.call-done.s_hbm = f32[640,2048]{1,0:T(8,128)} async-done(((f32[40,2048]{1,0:T(8,128)}), f32[640,2048]{1,0:T(8,128)}) %all-gather.2.cloned.1.call-update) | async-done | bytes 5242896 | tf_op jit(solution)/shard_map/all_gather | solution.py:276
  62.1 0.0 copy-start
  62.1 17.3 %shard_map.51 = bf16[32,18,128]{2,1,0:T(8,128)(2,1)S(1)} custom-call(s32[1]{0:T(128)} %bitcast.me_ref, f32[640,2048]{1,0:T(8,128)} %all-gather.2.cloned.1.call-done.s_hbm), custom_call_target="tpu_custom_call" | custom-call | tf_op jit(solution)/shard_map/pallas_call | solution.py:127
  79.4 20.3 %all_to_all.15.arrived_ref = bf16[32,18,128]{2,1,0:T(8,128)(2,1)S(1)} all-to-all(bf16[32,18,128]{2,1,0:T(8,128)(2,1)S(1)} %shard_map.51), channel_id=1, replica_groups=mesh['rep'=32,'fsdp'=16] {'rep'}, dimensions={0} | all-to-all | bytes 294912 | tf_op jit(solution)/shard_map/all_to_all | solution.py:263
  99.8 0.0 copy-done
  99.8 0.6 shard_map.52
  100.3 14.6 %all_to_all.16 = bf16[8,144,128]{2,1,0:T(8,128)(2,1)S(1)} all-to-all(bf16[8,144,128]{2,1,0:T(8,128)(2,1)S(1)} %shard_map.52), channel_id=1, replica_groups={{0,16,32,48,64,80,96,112},{128,144,160,176,192,208,224,240},{256,272,28..., dimensions={0} | all-to-all | bytes 589824 | tf_op jit(solution)/shard_map/all_to_all | solution.py:257
  114.9 0.2 broadcast_in_dim.14
  115.1 16.7 %all_to_all.17 = bf16[4,8,144,128]{3,2,1,0:T(8,128)(2,1)S(1)} all-to-all(bf16[4,8,144,128]{3,2,1,0:T(8,128)(2,1)S(1)} %broadcast_in_dim.14), channel_id=1, replica_groups={{0,128,256,384},{16,144,272,400},{32,160,288,416},{48,176,304,432},{64,..., dimensions={0} | all-to-all | bytes 2359296 | tf_op jit(solution)/shard_map/all_to_all | solution.py:257
  131.8 1.2 shard_map.53
Async XLA Ops:
  7.2 55.0 %all-gather.2.cloned.1.call-start = ((), (), s32[]{:S(2)}) async-start(), calls=%async_computation.3 | async-start | bytes 5570560 | tf_op jit(solution)/shard_map/all_gather | solution.py:276
  62.1 37.6 %copy-start = (s32[8]{0:T(128)S(1)}, s32[8]{0:T(128)}, u32[]{:S(2)}) copy-start(s32[8]{0:T(128)} %owners_ref.1) | copy-start | bytes 100
Sparse Core Ops, SparseCore 0:
  10.7 51.3 all-gather.1

commit v3 on v2

--- a/solution.py
+++ b/solution.py
@@ -17,8 +17,11 @@
 TALL = PAD * N_FSDP
 NX, NY = 4, 8
 N_REP = NX * NY
-HALF = OWN // 2
 CHUNK = 512
+SHARE = 8
+WIDE = COLS // SHARE
+SIDES = WIDE // 128
+TALL_PIECE = OWN * SIDES
 
 EPSILON = 1e-07
 MOMENTUM_BETA = 0.95
@@ -27,6 +30,14 @@
 QUINTIC_C = 2.0315
 
 f32, bf16 = jnp.float32, jnp.bfloat16
+
+
+def member(group):
+    return group // NY * 2 + group % 2
+
+
+def teams():
+    return [[x * NY + y + b for x in range(NX) for b in range(2)] for y in range(0, NY, 2)]
 
 
 def split(value):
@@ -113,20 +124,20 @@
     factor = 0.2 * math.sqrt(max(ROWS, COLS))
     for part in range(chunks):
         update = thin_product(mixed, (high_ref[part], low_ref[part])) * inverse * factor
-        for block in range(CHUNK // 128):
-            lane = part * (CHUNK // 128) + block
-            iy, left = lane // 2, lane % 2
-            for half in range(2):
-                ix = left * 2 + half
-                piece = update[half * HALF : (half + 1) * HALF, block * 128 : (block + 1) * 128]
-                u_ref[ix * NY + iy] = piece.astype(bf16)
+        for inner in range(CHUNK // WIDE):
+            lane = inner * WIDE
+            sides = [update[:OWN, lane + side * 128 : lane + (side + 1) * 128] for side in range(SIDES)]
+            piece = jnp.concatenate(sides, axis=0).astype(bf16)
+            for group in range(N_REP):
+                if member(group) == part * (CHUNK // WIDE) + inner:
+                    u_ref[group] = piece
 
 
 def orthogonal_rows(position, whole):
     chunks = COLS // CHUNK
     return pl.pallas_call(
         orthogonal_kernel,
-        out_shape=jax.ShapeDtypeStruct((N_REP, HALF, 128), bf16),
+        out_shape=jax.ShapeDtypeStruct((N_REP, TALL_PIECE, 128), bf16),
         in_specs=[
             pl.BlockSpec(memory_space=pltpu.SMEM),
             pl.BlockSpec(memory_space=pltpu.HBM),
@@ -145,37 +156,39 @@
 
 def choose_kernel(owners_ref, arrived_ref, out_ref, rows_ref):
     for mat in range(MATS):
-        rows_ref[pl.ds(mat, HALF, stride=MATS), :] = arrived_ref[owners_ref[mat]].astype(f32)
+        rows_ref[pl.ds(mat, TALL_PIECE, stride=MATS), :] = arrived_ref[owners_ref[mat]].astype(f32)
     rows = rows_ref[...].astype(bf16)
-    for copy in range(NY):
+    for copy in range(SHARE):
         out_ref[copy] = rows
 
 
 def choose(owners, arrived):
     return pl.pallas_call(
         choose_kernel,
-        out_shape=jax.ShapeDtypeStruct((NY, HALF * MATS, 128), bf16),
+        out_shape=jax.ShapeDtypeStruct((SHARE, TALL_PIECE * MATS, 128), bf16),
         in_specs=[pl.BlockSpec(memory_space=pltpu.SMEM), pl.BlockSpec(memory_space=pltpu.VMEM)],
         out_specs=pl.BlockSpec(memory_space=pltpu.VMEM),
-        scratch_shapes=[pltpu.VMEM((HALF * MATS, 128), f32)],
+        scratch_shapes=[pltpu.VMEM((TALL_PIECE * MATS, 128), f32)],
         compiler_params=pltpu.CompilerParams(vmem_limit_bytes=16 * 1024 * 1024),
     )(owners, arrived)
 
 
 def assemble_kernel(parts_ref, out_hbm, rows_ref, sems):
-    def store(half):
-        rows = pl.ds(half * HALF, HALF)
-        return pltpu.make_async_copy(rows_ref.at[rows], out_hbm.at[rows], sems.at[half])
-
-    for half in range(2):
-        for iy in range(NY):
-            for left in range(2):
-                lane = (iy * 2 + left) * 128
-                piece = parts_ref[2 * left + half, iy * HALF : (iy + 1) * HALF]
-                rows_ref[half * HALF : (half + 1) * HALF, :, lane : lane + 128] = piece
-        store(half).start()
-    for half in range(2):
-        store(half).wait()
+    half = OWN // 2
+
+    def store(step):
+        rows = pl.ds(step * half, half)
+        return pltpu.make_async_copy(rows_ref.at[rows], out_hbm.at[rows], sems.at[step])
+
+    for step in range(2):
+        for part in range(SHARE):
+            for side in range(SIDES):
+                lane = part * WIDE + side * 128
+                first = side * OWN + step * half
+                rows_ref[step * half : (step + 1) * half, :, lane : lane + 128] = parts_ref[part, first : first + half]
+        store(step).start()
+    for step in range(2):
+        store(step).wait()
 
 
 def assemble(parts):
@@ -253,18 +266,11 @@
     )(group, in_hbm(owners), in_hbm(grads), in_hbm(momentum))
 
 
-def exchange(copies, groups):
-    return lax.all_to_all(copies, "rep", split_axis=0, concat_axis=0, tiled=True, axis_index_groups=groups)
-
-
 def deliver(pieces, owners):
-    along_y = [[x * NY + y for y in range(NY)] for x in range(NX)]
-    along_x = [[x * NY + y for x in range(NX)] for y in range(NY)]
     arrived = lax.all_to_all(pieces, "rep", split_axis=0, concat_axis=0, tiled=True)
-    column = exchange(choose(owners, arrived), along_y)
-    copies = jnp.broadcast_to(column[None], (NX, *column.shape))
-    parts = exchange(copies, along_x)
-    rows = assemble(parts.reshape(NX, NY * HALF, MATS, 128))
+    copies = choose(owners, arrived)
+    parts = lax.all_to_all(copies, "rep", split_axis=0, concat_axis=0, tiled=True, axis_index_groups=teams())
+    rows = assemble(parts.reshape(SHARE, TALL_PIECE, MATS, 128))
     return rows.transpose(1, 0, 2)
 
 

time: 140 us -> 137 us (0.979)
  the two profiles are of different devices: /device:TPU:2 before, /device:TPU:8 now
where the time goes in v3:
time: 137 us; the launch traced here: 136 us
  waiting for transfers between devices  52.5 us (38%)
  blocking collectives  48.3 us (35%)
  Pallas kernels  21.5 us (16%)
  between operations  14.1 us (10%)
    all_gather x1, waiting for transfers between devices, shards(): whole = lax.all_gather(steered, 'fsdp', axis=0, tiled=True)  52.5 us
    all_to_all x1, blocking collectives, deliver(): lax.all_to_all(pieces, 'rep', split_axis=0, concat_axis=0, tiled=True)  29 us
    all_to_all x1, blocking collectives, deliver(): lax.all_to_all(copies, 'rep', split_axis=0, concat_axis=0, tiled=True, ax...  19.3 us
    pallas_call x1, Pallas kernels, orthogonal_rows(): pl.pallas_call(orthogonal_kernel, out_shape=jax.ShapeDtypeStruct((N_REP,...  17.2 us
  transfers between devices with their start and end apart: 1, of which 1 were waited for; matrix products, arithmetic and copies ran while one was open for 0% of the time, Pallas kernels for 0%

profile of v3, /device:TPU:8, one launch (start us, length us, event | category | flops | bytes accessed | tf_op | source)
XLA Modules:
  0.0 136.4 jit_solution(286482539039774794)
XLA Ops:
  7.2 0.0 all-gather.2.cloned.1.call-start
  7.2 2.4 %shard_map.50 = (f32[576,128]{1,0:T(8,128)}, f32[40,2048]{1,0:T(8,128)}) custom-call(s32[1]{0:T(128)} %bitcast.1.group_ref, s32[8]{0:T(128)} %owners_ref.1, bf16[36,8,2048]{2,1,0:T(8,128)(2,1)} %bitcast.8, f32[576,128]{1,0:T(8,128)} %bitcast.10), custom_call_target="tpu_custom_call" | custom-call | tf_op jit(solution)/shard_map/pallas_call | solution.py:250
  9.6 0.0 all-gather.2.cloned.1.call-update
  9.6 52.5 %all-gather.2.cloned.1.call-done.s_hbm = f32[640,2048]{1,0:T(8,128)} async-done(((f32[40,2048]{1,0:T(8,128)}), f32[640,2048]{1,0:T(8,128)}) %all-gather.2.cloned.1.call-update) | async-done | bytes 5242896 | tf_op jit(solution)/shard_map/all_gather | solution.py:282
  62.1 17.2 %shard_map.51 = bf16[32,72,128]{2,1,0:T(8,128)(2,1)S(1)} custom-call(s32[1]{0:T(128)} %bitcast.me_ref, f32[640,2048]{1,0:T(8,128)} %all-gather.2.cloned.1.call-done.s_hbm), custom_call_target="tpu_custom_call" | custom-call | tf_op jit(solution)/shard_map/pallas_call | solution.py:138
  79.3 0.0 copy-start
  79.3 29.0 %all_to_all.10.arrived_ref = bf16[32,72,128]{2,1,0:T(8,128)(2,1)S(1)} all-to-all(bf16[32,72,128]{2,1,0:T(8,128)(2,1)S(1)} %shard_map.51), channel_id=1, replica_groups=mesh['rep'=32,'fsdp'=16] {'rep'}, dimensions={0} | all-to-all | bytes 1179648 | tf_op jit(solution)/shard_map/all_to_all | solution.py:270
  108.4 0.0 copy-done
  108.4 0.7 shard_map.52
  109.1 19.3 %all_to_all.11 = bf16[8,576,128]{2,1,0:T(8,128)(2,1)S(1)} all-to-all(bf16[8,576,128]{2,1,0:T(8,128)(2,1)S(1)} %shard_map.52), channel_id=1, replica_groups={{0,16,128,144,256,272,384,400},{32,48,160,176,288,304,416,432},{64,80,1..., dimensions={0} | all-to-all | bytes 2359296 | tf_op jit(solution)/shard_map/all_to_all | solution.py:272
  128.4 1.2 shard_map.53
Async XLA Ops:
  7.2 54.9 %all-gather.2.cloned.1.call-start = ((), (), s32[]{:S(2)}) async-start(), calls=%async_computation.2 | async-start | bytes 5570560 | tf_op jit(solution)/shard_map/all_gather | solution.py:282
  79.3 29.1 %copy-start = (s32[8]{0:T(128)S(1)}, s32[8]{0:T(128)}, u32[]{:S(2)}) copy-start(s32[8]{0:T(128)} %owners_ref.1) | copy-start | bytes 100
Sparse Core Ops, SparseCore 0:
  10.7 51.3 all-gather.1

commit v4 on v3

--- a/solution.py
+++ b/solution.py
@@ -14,7 +14,8 @@
 N_FSDP = 16
 OWN = ROWS // N_FSDP
 PAD = 40
-TALL = PAD * N_FSDP
+STEM = 32
+TAIL = OWN - STEM
 NX, NY = 4, 8
 N_REP = NX * NY
 CHUNK = 512
@@ -74,20 +75,31 @@
     return first[:PAD] + (first[PAD:] + second[:PAD])
 
 
-def orthogonal_kernel(me_ref, s_hbm, u_ref, s_ref, high_ref, low_ref, rows_ref, sems):
+def orthogonal_kernel(me_ref, s_hbm, u_ref, stem_ref, tail_ref, high_ref, low_ref, sems):
     chunks = COLS // CHUNK
+    blocks = CHUNK // 128
 
     def fetch(part):
-        lanes = pl.ds(part * CHUNK, CHUNK)
-        return pltpu.make_async_copy(s_hbm.at[:, lanes], s_ref.at[part], sems.at[part])
-
+        rows = pl.ds(part * blocks * STEM, blocks * STEM)
+        return pltpu.make_async_copy(s_hbm.at[:, rows, :], stem_ref.at[part], sems.at[part])
+
+    tails = pl.ds(COLS // 128 * STEM, COLS // 128 * TAIL)
+    fetch_tails = pltpu.make_async_copy(s_hbm.at[:, tails, :], tail_ref, sems.at[chunks])
+    fetch_tails.start()
     for part in range(chunks):
         fetch(part).start()
+    fetch_tails.wait()
     gram = None
     cross = None
     for part in range(chunks):
         fetch(part).wait()
-        high, low = split(s_ref[part])
+        columns = []
+        for inner in range(blocks):
+            stem = stem_ref[part, :, inner * STEM : (inner + 1) * STEM, :].reshape(N_FSDP * STEM, 128)
+            first = (part * blocks + inner) * TAIL
+            tail = [tail_ref[device, first : first + TAIL, :] for device in range(N_FSDP)]
+            columns.append(jnp.concatenate([stem] + tail, axis=0))
+        high, low = split(jnp.concatenate(columns, axis=1))
         high_ref[part] = high
         low_ref[part] = low
         more_cross, more = dot_nt(high, low), dot_nt(high, high)
@@ -95,32 +107,38 @@
         gram = more if part == 0 else gram + more
     gram = gram + (cross + cross.T)
 
-    row = lax.broadcasted_iota(jnp.int32, (TALL, TALL), 0)
-    col = lax.broadcasted_iota(jnp.int32, (TALL, TALL), 1)
+    row = lax.broadcasted_iota(jnp.int32, (ROWS, ROWS), 0)
+    col = lax.broadcasted_iota(jnp.int32, (ROWS, ROWS), 1)
     diagonal = row == col
     total = jnp.sum(jnp.where(diagonal, gram, 0.0), axis=(0, 1), keepdims=True)
     inverse = 1.0 / (jnp.sqrt(total) + EPSILON)
-    start = pl.multiple_of(me_ref[0] * PAD, 8)
-
-    def poly(gram, squared):
-        return jnp.where(diagonal, QUINTIC_A, 0.0) + QUINTIC_B * gram + QUINTIC_C * squared
-
     g0 = gram * inverse * inverse
     g0s = split(g0)
-    q1s = split(poly(g0, square(g0s)))
-    g1 = product(g0s, split(square(q1s)))
-    g1s = split(g1)
-    q2 = poly(g1, square(g1s))
-    q2s = split(q2)
-    rows_ref[...] = q2
-    mixed = thin_product(rows_ref[pl.ds(start, PAD), :], q1s)
+    q1s = split(jnp.where(diagonal, QUINTIC_A, 0.0) + QUINTIC_B * g0 + QUINTIC_C * square(g0s))
+    g1s = split(product(g0s, split(square(q1s))))
+
+    def by_g1(rows):
+        return thin_product(rows, g1s)
+
+    def quintic(rows, once, twice):
+        return QUINTIC_A * rows + QUINTIC_B * once + QUINTIC_C * twice
+
+    def by_q2(rows):
+        once = by_g1(rows)
+        return quintic(rows, once, by_g1(once))
 
     def by_g2(rows):
-        return thin_product(thin_product(thin_product(rows, g1s), q2s), q2s)
-
+        return by_q2(by_q2(by_g1(rows)))
+
+    local = lax.broadcasted_iota(jnp.int32, (PAD, ROWS), 0)
+    here = lax.broadcasted_iota(jnp.int32, (PAD, ROWS), 1)
+    in_stem = me_ref[0] * STEM + local
+    in_tail = N_FSDP * STEM + me_ref[0] * TAIL + local - STEM
+    own = jnp.where(local < STEM, in_stem, jnp.where(local < OWN, in_tail, -1))
+    unit = jnp.where(own == here, 1.0, 0.0)
+    mixed = thin_product(by_q2(unit), q1s)
     once = by_g2(mixed)
-    twice = by_g2(once)
-    mixed = QUINTIC_A * mixed + QUINTIC_B * once + QUINTIC_C * twice
+    mixed = quintic(mixed, once, by_g2(once))
     factor = 0.2 * math.sqrt(max(ROWS, COLS))
     for part in range(chunks):
         update = thin_product(mixed, (high_ref[part], low_ref[part])) * inverse * factor
@@ -144,11 +162,11 @@
         ],
         out_specs=pl.BlockSpec(memory_space=pltpu.VMEM),
         scratch_shapes=[
-            pltpu.VMEM((chunks, TALL, CHUNK), f32),
-            pltpu.VMEM((chunks, TALL, CHUNK), bf16),
-            pltpu.VMEM((chunks, TALL, CHUNK), bf16),
-            pltpu.VMEM((TALL, TALL), f32),
-            pltpu.SemaphoreType.DMA((chunks,)),
+            pltpu.VMEM((chunks, N_FSDP, CHUNK // 128 * STEM, 128), f32),
+            pltpu.VMEM((N_FSDP, COLS // 128 * TAIL, 128), f32),
+            pltpu.VMEM((chunks, ROWS, CHUNK), bf16),
+            pltpu.VMEM((chunks, ROWS, CHUNK), bf16),
+            pltpu.SemaphoreType.DMA((chunks + 1,)),
         ],
         compiler_params=pltpu.CompilerParams(vmem_limit_bytes=48 * 1024 * 1024),
     )(position, whole)
@@ -219,7 +237,6 @@
     fetch_momentum.start()
     for part in range(chunks):
         fetch(part).start()
-    steered_ref[OWN:, :] = jnp.zeros((PAD - OWN, COLS), f32)
     fetch_owners.wait()
     owns_one = owners_ref[0] == group_ref[0]
     chosen = 0
@@ -238,7 +255,10 @@
         held_state = momentum_ref[pl.ds(block, OWN, stride=blocks), :]
         renewed = jnp.where(owns_one, MOMENTUM_BETA * held_state + gradient, held_state)
         renewed_ref[pl.ds(block, OWN, stride=blocks), :] = renewed
-        steered_ref[:OWN, block * 128 : (block + 1) * 128] = gradient + MOMENTUM_BETA * renewed
+        steered = gradient + MOMENTUM_BETA * renewed
+        steered_ref[block * STEM : (block + 1) * STEM, :] = steered[:STEM]
+        first = blocks * STEM + block * TAIL
+        steered_ref[first : first + TAIL, :] = steered[STEM:]
 
 
 def in_hbm(value):
@@ -253,7 +273,7 @@
         out_specs=[pl.BlockSpec(memory_space=pltpu.VMEM)] * 2,
         out_shape=[
             jax.ShapeDtypeStruct((OWN * COLS // 128, 128), f32),
-            jax.ShapeDtypeStruct((PAD, COLS), f32),
+            jax.ShapeDtypeStruct((OWN * COLS // 128, 128), f32),
         ],
         scratch_shapes=[
             pltpu.SMEM((MATS,), jnp.int32),
@@ -279,7 +299,7 @@
     position = lax.axis_index("fsdp").astype(jnp.int32)[None]
     flat = momentum.reshape(OWN * COLS // 128, 128)
     renewed, steered = steer(owners, group, grads.transpose(1, 0, 2), flat)
-    whole = lax.all_gather(steered, "fsdp", axis=0, tiled=True)
+    whole = lax.all_gather(steered, "fsdp")
     pieces = orthogonal_rows(position, in_hbm(whole))
     update = deliver(pieces, owners)
     return (update, renewed.reshape(1, OWN, COLS))

time: 137 us -> 135 us (0.985)
  no operation moved by 1% of the time
where the time goes in v4:
time: 135 us
  waiting for transfers between devices  51.9 us (38%)
  blocking collectives  48.3 us (36%)
  Pallas kernels  20.5 us (15%)
  between operations  14.1 us (10%)
    all_gather x1, waiting for transfers between devices, shards(): whole = lax.all_gather(steered, 'fsdp')  51.9 us
    all_to_all x1, blocking collectives, deliver(): lax.all_to_all(pieces, 'rep', split_axis=0, concat_axis=0, tiled=True)  29.1 us
    all_to_all x1, blocking collectives, deliver(): lax.all_to_all(copies, 'rep', split_axis=0, concat_axis=0, tiled=True, ax...  19.2 us
    pallas_call x1, Pallas kernels, orthogonal_rows(): pl.pallas_call(orthogonal_kernel, out_shape=jax.ShapeDtypeStruct((N_REP,...  16.3 us
  transfers between devices with their start and end apart: 1, of which 1 were waited for; matrix products, arithmetic and copies ran while one was open for 0% of the time, Pallas kernels for 0%

profile of v4, /device:TPU:8, one launch (start us, length us, event | category | flops | bytes accessed | tf_op | source)
XLA Modules:
  0.0 134.8 jit_solution(18121028726481665979)
XLA Ops:
  7.2 0.0 all-gather.3.cloned.1.call-start
  7.2 2.3 %shard_map.50 = (f32[576,128]{1,0:T(8,128)}, f32[576,128]{1,0:T(8,128)}) custom-call(s32[1]{0:T(128)} %bitcast.1.group_ref, s32[8]{0:T(128)} %owners_ref.1, bf16[36,8,2048]{2,1,0:T(8,128)(2,1)} %bitcast.10, f32[576,128]{1,0:T(8,128)} %bitcast.12), custom_call_target="tpu_custom_call" | custom-call | tf_op jit(solution)/shard_map/pallas_call | solution.py:270
  9.6 0.0 all-gather.3.cloned.1.call-update
  9.6 51.9 %all-gather.3.cloned.1.call-done = f32[9216,128]{1,0:T(8,128)} async-done(((f32[576,128]{1,0:T(8,128)}), f32[9216,128]{1,0:T(8,128)}) %all-gather.3.cloned.1.call-update) | async-done | bytes 4718608 | tf_op jit(solution)/shard_map/all_gather | solution.py:302
  61.4 16.3 %shard_map.51 = bf16[32,72,128]{2,1,0:T(8,128)(2,1)S(1)} custom-call(s32[1]{0:T(128)} %bitcast.me_ref, f32[16,576,128]{2,1,0:T(8,128)} %bitcast.9), custom_call_target="tpu_custom_call" | custom-call | tf_op jit(solution)/shard_map/pallas_call | solution.py:156
  77.7 0.0 copy-start
  77.7 29.1 %all_to_all.10.arrived_ref = bf16[32,72,128]{2,1,0:T(8,128)(2,1)S(1)} all-to-all(bf16[32,72,128]{2,1,0:T(8,128)(2,1)S(1)} %shard_map.51), channel_id=1, replica_groups=mesh['rep'=32,'fsdp'=16] {'rep'}, dimensions={0} | all-to-all | bytes 1179648 | tf_op jit(solution)/shard_map/all_to_all | solution.py:290
  106.8 0.0 copy-done
  106.8 0.7 shard_map.52
  107.5 19.2 %all_to_all.11 = bf16[8,576,128]{2,1,0:T(8,128)(2,1)S(1)} all-to-all(bf16[8,576,128]{2,1,0:T(8,128)(2,1)S(1)} %shard_map.52), channel_id=1, replica_groups={{0,16,128,144,256,272,384,400},{32,48,160,176,288,304,416,432},{64,80,1..., dimensions={0} | all-to-all | bytes 2359296 | tf_op jit(solution)/shard_map/all_to_all | solution.py:292
  126.7 1.2 shard_map.53
Async XLA Ops:
  7.2 54.3 %all-gather.3.cloned.1.call-start = ((), (), s32[]{:S(2)}) async-start(), calls=%async_computation.2 | async-start | bytes 5013504 | tf_op jit(solution)/shard_map/all_gather | solution.py:302
  77.7 29.1 %copy-start = (s32[8]{0:T(128)S(1)}, s32[8]{0:T(128)}, u32[]{:S(2)}) copy-start(s32[8]{0:T(128)} %owners_ref.1) | copy-start | bytes 100
Sparse Core Ops, SparseCore 0:
  10.7 50.7 all-gather.2

commit v5 on v4

--- a/solution.py
+++ b/solution.py
@@ -14,6 +14,7 @@
 N_FSDP = 16
 OWN = ROWS // N_FSDP
 PAD = 40
+SIDE = 256
 STEM = 32
 TAIL = OWN - STEM
 NX, NY = 4, 8
@@ -57,13 +58,33 @@
 
 def product(left, right):
     (lh, ll), (rh, rl) = left, right
-    return (dot(lh, rl) + dot(ll, rh)) + dot(lh, rh)
+    deep = 2 * SIDE
+    ends = jnp.concatenate([lh[:, deep:], ll[:, deep:], lh[:, deep:]], axis=1)
+    tops = jnp.concatenate([rl[deep:], rh[deep:], rh[deep:]], axis=0)
+    lh, ll, rh, rl = lh[:, :deep], ll[:, :deep], rh[:deep], rl[:deep]
+    return ((dot(lh, rl) + dot(ll, rh)) + dot(ends, tops)) + dot(lh, rh)
+
+
+def mirror(top, middle, bottom):
+    first = jnp.concatenate([top, bottom[:, :SIDE].T], axis=1)
+    second = jnp.concatenate([top[:, SIDE:].T, middle, bottom[:, SIDE : 2 * SIDE].T], axis=1)
+    return jnp.concatenate([first, second, bottom], axis=0)
+
+
+BLOCKS = ((0, SIDE, 0, 2 * SIDE), (SIDE, 2 * SIDE, SIDE, 2 * SIDE), (2 * SIDE, ROWS, 0, ROWS))
+
+
+def symmetric_product(left, right):
+    (lh, ll), (rh, rl) = left, right
+    return mirror(
+        *[product((lh[a:b], ll[a:b]), (rh[:, c:d], rl[:, c:d])) for a, b, c, d in BLOCKS]
+    )
 
 
 def square(halves):
     high, low = halves
     cross = dot(high, low)
-    return (cross + cross.T) + dot(high, high)
+    return (cross + cross.T) + mirror(*[dot(high[a:b], high[:, c:d]) for a, b, c, d in BLOCKS])
 
 
 def thin_product(rows, halves):
@@ -71,8 +92,8 @@
     kept = rows.astype(bf16).astype(f32)
     stacked = jnp.concatenate([kept, rows - kept], axis=0).astype(bf16)
     first = dot(stacked, high)
-    second = dot(stacked, low)
-    return first[:PAD] + (first[PAD:] + second[:PAD])
+    second = dot(stacked[:PAD], low)
+    return first[:PAD] + (first[PAD:] + second)
 
 
 def orthogonal_kernel(me_ref, s_hbm, u_ref, stem_ref, tail_ref, high_ref, low_ref, sems):
@@ -115,7 +136,7 @@
     g0 = gram * inverse * inverse
     g0s = split(g0)
     q1s = split(jnp.where(diagonal, QUINTIC_A, 0.0) + QUINTIC_B * g0 + QUINTIC_C * square(g0s))
-    g1s = split(product(g0s, split(square(q1s))))
+    g1s = split(symmetric_product(g0s, split(square(q1s))))
 
     def by_g1(rows):
         return thin_product(rows, g1s)

time: 135 us -> 134 us (level)
  Pallas kernels: 20.5 us -> 19 us
    pallas_call x1, Pallas kernels: 16.3 us -> 14.8 us  [orthogonal_rows(): pl.pallas_call(orthogonal_kernel, out_shape=jax.ShapeDtypeStruct((N_REP,...]
where the time goes in v5:
time: 134 us; the launch traced here: 133 us
  waiting for transfers between devices  51.9 us (39%)
  blocking collectives  48.3 us (36%)
  Pallas kernels  19 us (14%)
  between operations  14.1 us (11%)
    all_gather x1, waiting for transfers between devices, shards(): whole = lax.all_gather(steered, 'fsdp')  51.9 us
    all_to_all x1, blocking collectives, deliver(): lax.all_to_all(pieces, 'rep', split_axis=0, concat_axis=0, tiled=True)  29 us
    all_to_all x1, blocking collectives, deliver(): lax.all_to_all(copies, 'rep', split_axis=0, concat_axis=0, tiled=True, ax...  19.2 us
    pallas_call x1, Pallas kernels, orthogonal_rows(): pl.pallas_call(orthogonal_kernel, out_shape=jax.ShapeDtypeStruct((N_REP,...  14.8 us
  transfers between devices with their start and end apart: 1, of which 1 were waited for; matrix products, arithmetic and copies ran while one was open for 0% of the time, Pallas kernels for 0%

profile of v5, /device:TPU:8, one launch (start us, length us, event | category | flops | bytes accessed | tf_op | source)
XLA Modules:
  0.0 133.3 jit_solution(1069009140848979449)
XLA Ops:
  7.2 0.0 all-gather.3.cloned.1.call-start
  7.2 2.3 %shard_map.50 = (f32[576,128]{1,0:T(8,128)}, f32[576,128]{1,0:T(8,128)}) custom-call(s32[1]{0:T(128)} %bitcast.1.group_ref, s32[8]{0:T(128)} %owners_ref.1, bf16[36,8,2048]{2,1,0:T(8,128)(2,1)} %bitcast.10, f32[576,128]{1,0:T(8,128)} %bitcast.12), custom_call_target="tpu_custom_call" | custom-call | tf_op jit(solution)/shard_map/pallas_call | solution.py:291
  9.6 0.0 all-gather.3.cloned.1.call-update
  9.6 51.9 %all-gather.3.cloned.1.call-done = f32[9216,128]{1,0:T(8,128)} async-done(((f32[576,128]{1,0:T(8,128)}), f32[9216,128]{1,0:T(8,128)}) %all-gather.3.cloned.1.call-update) | async-done | bytes 4718608 | tf_op jit(solution)/shard_map/all_gather | solution.py:323
  61.4 14.8 %shard_map.51 = bf16[32,72,128]{2,1,0:T(8,128)(2,1)S(1)} custom-call(s32[1]{0:T(128)} %bitcast.me_ref, f32[16,576,128]{2,1,0:T(8,128)} %bitcast.9), custom_call_target="tpu_custom_call" | custom-call | tf_op jit(solution)/shard_map/pallas_call | solution.py:177
  76.3 0.0 copy-start
  76.3 29.0 %all_to_all.10.arrived_ref = bf16[32,72,128]{2,1,0:T(8,128)(2,1)S(1)} all-to-all(bf16[32,72,128]{2,1,0:T(8,128)(2,1)S(1)} %shard_map.51), channel_id=1, replica_groups=mesh['rep'=32,'fsdp'=16] {'rep'}, dimensions={0} | all-to-all | bytes 1179648 | tf_op jit(solution)/shard_map/all_to_all | solution.py:311
  105.3 0.0 copy-done
  105.3 0.7 shard_map.52
  106.0 19.2 %all_to_all.11 = bf16[8,576,128]{2,1,0:T(8,128)(2,1)S(1)} all-to-all(bf16[8,576,128]{2,1,0:T(8,128)(2,1)S(1)} %shard_map.52), channel_id=1, replica_groups={{0,16,128,144,256,272,384,400},{32,48,160,176,288,304,416,432},{64,80,1..., dimensions={0} | all-to-all | bytes 2359296 | tf_op jit(solution)/shard_map/all_to_all | solution.py:313
  125.3 1.2 shard_map.53
Async XLA Ops:
  7.2 54.3 %all-gather.3.cloned.1.call-start = ((), (), s32[]{:S(2)}) async-start(), calls=%async_computation.2 | async-start | bytes 5013504 | tf_op jit(solution)/shard_map/all_gather | solution.py:323
  76.3 29.1 %copy-start = (s32[8]{0:T(128)S(1)}, s32[8]{0:T(128)}, u32[]{:S(2)}) copy-start(s32[8]{0:T(128)} %owners_ref.1) | copy-start | bytes 100
Sparse Core Ops, SparseCore 0:
  10.7 50.7 all-gather.2

commit v6 on v5

--- a/solution.py
+++ b/solution.py
@@ -96,7 +96,7 @@
     return first[:PAD] + (first[PAD:] + second)
 
 
-def orthogonal_kernel(me_ref, s_hbm, u_ref, stem_ref, tail_ref, high_ref, low_ref, sems):
+def orthogonal_kernel(me_ref, s_hbm, greeting_hbm, meeting_hbm, u_ref, stem_ref, tail_ref, high_ref, low_ref, sems):
     chunks = COLS // CHUNK
     blocks = CHUNK // 128
 
@@ -172,7 +172,7 @@
                     u_ref[group] = piece
 
 
-def orthogonal_rows(position, whole):
+def orthogonal_rows(position, whole, greeting, meeting):
     chunks = COLS // CHUNK
     return pl.pallas_call(
         orthogonal_kernel,
@@ -180,6 +180,8 @@
         in_specs=[
             pl.BlockSpec(memory_space=pltpu.SMEM),
             pl.BlockSpec(memory_space=pltpu.HBM),
+            pl.BlockSpec(memory_space=pl.ANY),
+            pl.BlockSpec(memory_space=pl.ANY),
         ],
         out_specs=pl.BlockSpec(memory_space=pltpu.VMEM),
         scratch_shapes=[
@@ -190,7 +192,7 @@
             pltpu.SemaphoreType.DMA((chunks + 1,)),
         ],
         compiler_params=pltpu.CompilerParams(vmem_limit_bytes=48 * 1024 * 1024),
-    )(position, whole)
+    )(position, whole, greeting, meeting)
 
 
 def choose_kernel(owners_ref, arrived_ref, out_ref, rows_ref):
@@ -321,7 +323,16 @@
     flat = momentum.reshape(OWN * COLS // 128, 128)
     renewed, steered = steer(owners, group, grads.transpose(1, 0, 2), flat)
     whole = lax.all_gather(steered, "fsdp")
-    pieces = orthogonal_rows(position, in_hbm(whole))
+    greeting = lax.all_to_all(renewed[: N_REP * 8].reshape(N_REP, 8, 128), "rep", split_axis=0, concat_axis=0, tiled=True)
+    meeting = lax.all_to_all(
+        renewed[: SHARE * 8].reshape(SHARE, 8, 128),
+        "rep",
+        split_axis=0,
+        concat_axis=0,
+        tiled=True,
+        axis_index_groups=teams(),
+    )
+    pieces = orthogonal_rows(position, in_hbm(whole), greeting, meeting)
     update = deliver(pieces, owners)
     return (update, renewed.reshape(1, OWN, COLS))
 

time: 134 us -> 134 us (level)
  waiting for transfers between devices: 51.9 us -> 34.7 us
  starting transfers between devices: 0.04 us -> 14.2 us
  local copies, waits for them, and re-layouts: 0.01 us -> 2.95 us
    all_gather x1, waiting for transfers between devices: 51.9 us -> 21.7 us  [shards(): whole = lax.all_gather(steered, 'fsdp')]
    all_to_all x0 -> x2, starting transfers between devices: none -> 14.1 us  [the longest x1 9.07 us: shards(): lax.all_to_all(renewed[:SHARE * 8].reshape(SHARE, 8, 128), 'rep', split_a...]
    all_to_all x0 -> x2, waiting for transfers between devices: none -> 13 us  [the longest x1 9.66 us: shards(): lax.all_to_all(renewed[:N_REP * 8].reshape(N_REP, 8, 128), 'rep', split_a...]
    reshape x0 -> x2, local copies, waits for them, and re-layouts: none -> 2.94 us  [the longest x1 1.57 us: shards(): renewed[:N_REP * 8].reshape(N_REP, 8, 128)]
  transfers between devices with their start and end apart: 1 -> 3, of which waited for: 1 -> 3; matrix products, arithmetic and copies ran while one was open for 0% -> 2% of each run, Pallas kernels for 0% -> 0%
where the time goes in v6:
time: 134 us; the launch traced here: 133 us
  blocking collectives  48.4 us (36%)
  waiting for transfers between devices  34.7 us (26%)
  Pallas kernels  19 us (14%)
  starting transfers between devices  14.2 us (11%)
  between operations  14.1 us (11%)
  local copies, waits for them, and re-layouts  2.95 us (2%)
    all_to_all x1, blocking collectives, deliver(): lax.all_to_all(pieces, 'rep', split_axis=0, concat_axis=0, tiled=True)  29.1 us
    all_gather x1, waiting for transfers between devices, shards(): whole = lax.all_gather(steered, 'fsdp')  21.7 us
    all_to_all x1, blocking collectives, deliver(): lax.all_to_all(copies, 'rep', split_axis=0, concat_axis=0, tiled=True, ax...  19.3 us
    pallas_call x1, Pallas kernels, orthogonal_rows(): pl.pallas_call(orthogonal_kernel, out_shape=jax.ShapeDtypeStruct((N_REP,...  14.8 us
    all_to_all x1, waiting for transfers between devices, shards(): lax.all_to_all(renewed[:N_REP * 8].reshape(N_REP, 8, 128), 'rep', split_a...  9.66 us
    all_to_all x1, starting transfers between devices, shards(): lax.all_to_all(renewed[:SHARE * 8].reshape(SHARE, 8, 128), 'rep', split_a...  9.07 us
    all_to_all x1, starting transfers between devices, shards(): lax.all_to_all(renewed[:N_REP * 8].reshape(N_REP, 8, 128), 'rep', split_a...  5.05 us
    all_to_all x1, waiting for transfers between devices, shards(): lax.all_to_all(renewed[:SHARE * 8].reshape(SHARE, 8, 128), 'rep', split_a...  3.35 us
  transfers between devices with their start and end apart: 3, of which 3 were waited for; matrix products, arithmetic and copies ran while one was open for 2% of the time, Pallas kernels for 0%

profile of v6, /device:TPU:8, one launch (start us, length us, event | category | flops | bytes accessed | tf_op | source)
XLA Modules:
  0.0 133.4 jit_solution(5063635233781969881)
XLA Ops:
  7.2 0.0 all-gather.3.cloned.1.call-start
  7.2 2.3 %shard_map.50 = (f32[576,128]{1,0:T(8,128)}, f32[576,128]{1,0:T(8,128)}) custom-call(s32[1]{0:T(128)} %bitcast.1.group_ref, s32[8]{0:T(128)} %owners_ref.1, bf16[36,8,2048]{2,1,0:T(8,128)(2,1)} %bitcast.14, f32[576,128]{1,0:T(8,128)} %bitcast.16), custom_call_target="tpu_custom_call" | custom-call | tf_op jit(solution)/shard_map/pallas_call | solution.py:293
  9.6 0.0 all-gather.3.cloned.1.call-update
  9.6 1.4 %slice_bitcast_fusion.1 = f32[8,8,128]{2,1,0:T(8,128)} fusion(f32[576,128]{1,0:T(8,128)} %get-tuple-element.5), kind=kLoop, calls=%fused_computation.1 | loop fusion | bytes 65536 | tf_op jit(solution)/shard_map/reshape | solution.py:328
  11.0 9.1 %all-to-all-start.1 = ((f32[8,8,128]{2,1,0:T(8,128)}), f32[8,8,128]{2,1,0:T(8,128)S(1)}, u32[]{:S(2)}, u32[]{:S(2)}) async-start(f32[8,8,128]{2,1,0:T(8,128)} %slice_bitcast_fusion.1), calls=%async_computation.1 | async-start | bytes 65536 | tf_op jit(solution)/shard_map/all_to_all | solution.py:327
  20.0 1.6 %slice_bitcast_fusion = f32[32,8,128]{2,1,0:T(8,128)} fusion(f32[576,128]{1,0:T(8,128)} %get-tuple-element.5), kind=kLoop, calls=%fused_computation | loop fusion | bytes 262144 | tf_op jit(solution)/shard_map/reshape | solution.py:326
  21.6 3.3 %all-to-all-done.1.meeting_hbm = f32[8,8,128]{2,1,0:T(8,128)S(1)} async-done(((f32[8,8,128]{2,1,0:T(8,128)}), f32[8,8,128]{2,1,0:T(8,128)S(1)}, u32[]{:S(2)}, u32[]{:S(2)}) %all-to-all-start.1) | async-done | bytes 32800 | tf_op jit(solution)/shard_map/all_to_all | solution.py:327
  24.9 5.0 %all-to-all-start = ((f32[32,8,128]{2,1,0:T(8,128)}), f32[32,8,128]{2,1,0:T(8,128)S(1)}, u32[]{:S(2)}, u32[]{:S(2)}) async-start(f32[32,8,128]{2,1,0:T(8,128)} %slice_bitcast_fusion), calls=%async_computation | async-start | bytes 262144 | tf_op jit(solution)/shard_map/all_to_all | solution.py:326
  30.0 9.7 %all-to-all-done.greeting_hbm = f32[32,8,128]{2,1,0:T(8,128)S(1)} async-done(((f32[32,8,128]{2,1,0:T(8,128)}), f32[32,8,128]{2,1,0:T(8,128)S(1)}, u32[]{:S(2)}, u32[]{:S(2)}) %all-to-all-start) | async-done | bytes 131104 | tf_op jit(solution)/shard_map/all_to_all | solution.py:326
  39.7 21.7 %all-gather.3.cloned.1.call-done = f32[9216,128]{1,0:T(8,128)} async-done(((f32[576,128]{1,0:T(8,128)}), f32[9216,128]{1,0:T(8,128)}) %all-gather.3.cloned.1.call-update) | async-done | bytes 4718608 | tf_op jit(solution)/shard_map/all_gather | solution.py:325
  61.4 14.8 %shard_map.51 = bf16[32,72,128]{2,1,0:T(8,128)(2,1)S(1)} custom-call(s32[1]{0:T(128)} %bitcast.me_ref, f32[16,576,128]{2,1,0:T(8,128)} %bitcast.13, f32[32,8,128]{2,1,0:T(8,128)S(1)} %all-to-all-done.greeting_hbm, f32[8,8,128]{2,1,0:T(8,128)S(1)} %all-to-all-done.1.meeting_hbm), custom_call_target="tpu_custom_call" | custom-call | tf_op jit(solution)/shard_map/pallas_call | solution.py:177
  76.2 0.0 copy-start
  76.2 29.1 %all_to_all.20.arrived_ref = bf16[32,72,128]{2,1,0:T(8,128)(2,1)S(1)} all-to-all(bf16[32,72,128]{2,1,0:T(8,128)(2,1)S(1)} %shard_map.51), channel_id=1, replica_groups=mesh['rep'=32,'fsdp'=16] {'rep'}, dimensions={0} | all-to-all | bytes 1179648 | tf_op jit(solution)/shard_map/all_to_all | solution.py:313
  105.3 0.0 copy-done
  105.4 0.7 shard_map.52
  106.1 19.3 %all_to_all.21 = bf16[8,576,128]{2,1,0:T(8,128)(2,1)S(1)} all-to-all(bf16[8,576,128]{2,1,0:T(8,128)(2,1)S(1)} %shard_map.52), channel_id=1, replica_groups={{0,16,128,144,256,272,384,400},{32,48,160,176,288,304,416,432},{64,80,1..., dimensions={0} | all-to-all | bytes 2359296 | tf_op jit(solution)/shard_map/all_to_all | solution.py:315
  125.3 1.2 shard_map.53
Async XLA Ops:
  7.2 54.2 %all-gather.3.cloned.1.call-start = ((), (), s32[]{:S(2)}) async-start(), calls=%async_computation.4 | async-start | bytes 5013504 | tf_op jit(solution)/shard_map/all_gather | solution.py:325
  11.0 14.0 %all-to-all-start.1 = ((f32[8,8,128]{2,1,0:T(8,128)}), f32[8,8,128]{2,1,0:T(8,128)S(1)}, u32[]{:S(2)}, u32[]{:S(2)}) async-start(f32[8,8,128]{2,1,0:T(8,128)} %slice_bitcast_fusion.1), calls=%async_computation.1 | async-start | bytes 65536 | tf_op jit(solution)/shard_map/all_to_all | solution.py:327
  24.9 14.7 %all-to-all-start = ((f32[32,8,128]{2,1,0:T(8,128)}), f32[32,8,128]{2,1,0:T(8,128)S(1)}, u32[]{:S(2)}, u32[]{:S(2)}) async-start(f32[32,8,128]{2,1,0:T(8,128)} %slice_bitcast_fusion), calls=%async_computation | async-start | bytes 262144 | tf_op jit(solution)/shard_map/all_to_all | solution.py:326
  76.2 29.2 %copy-start = (s32[8]{0:T(128)S(1)}, s32[8]{0:T(128)}, u32[]{:S(2)}) copy-start(s32[8]{0:T(128)} %owners_ref.1) | copy-start | bytes 100
Sparse Core Ops, SparseCore 0:
  10.7 50.6 all-gather.2

commit v7 on v5

--- a/solution.py
+++ b/solution.py
@@ -243,7 +243,7 @@
 
 def steer_kernel(
     group_ref, owners_hbm, grads_hbm, momentum_hbm, renewed_ref, steered_ref,
-    owners_ref, grads_ref, momentum_ref, wide_ref, sems,
+    owners_ref, grads_ref, momentum_ref, wide_ref, fresh_ref, sems,
 ):
     blocks = COLS // 128
     chunks = COLS // CHUNK
@@ -253,7 +253,8 @@
         return pltpu.make_async_copy(grads_hbm.at[:, :, lanes], grads_ref.at[part], sems.at[part])
 
     fetch_owners = pltpu.make_async_copy(owners_hbm, owners_ref, sems.at[chunks])
-    fetch_momentum = pltpu.make_async_copy(momentum_hbm, momentum_ref, sems.at[chunks + 1])
+    held_rows = pl.ds(0, OWN * blocks)
+    fetch_momentum = pltpu.make_async_copy(momentum_hbm, momentum_ref.at[held_rows], sems.at[chunks + 1])
     fetch_owners.start()
     fetch_momentum.start()
     for part in range(chunks):
@@ -271,15 +272,16 @@
         if inner == 0:
             fetch(part).wait()
         wide = grads_ref[part, :, :, inner * 128 : (inner + 1) * 128].astype(f32)
-        wide_ref[block] = wide.reshape(OWN * MATS, 128)
-        gradient = wide_ref[block, pl.ds(chosen, OWN, stride=MATS), :]
-        held_state = momentum_ref[pl.ds(block, OWN, stride=blocks), :]
+        wide_ref[block, : OWN * MATS, :] = wide.reshape(OWN * MATS, 128)
+        gradient = wide_ref[block, pl.ds(chosen, PAD, stride=MATS), :]
+        held_state = momentum_ref[pl.ds(block, PAD, stride=blocks), :]
         renewed = jnp.where(owns_one, MOMENTUM_BETA * held_state + gradient, held_state)
-        renewed_ref[pl.ds(block, OWN, stride=blocks), :] = renewed
+        fresh_ref[pl.ds(block, PAD, stride=blocks), :] = renewed
         steered = gradient + MOMENTUM_BETA * renewed
         steered_ref[block * STEM : (block + 1) * STEM, :] = steered[:STEM]
         first = blocks * STEM + block * TAIL
-        steered_ref[first : first + TAIL, :] = steered[STEM:]
+        steered_ref[first : first + TAIL, :] = steered[STEM:OWN]
+    renewed_ref[...] = fresh_ref[: OWN * blocks, :]
 
 
 def in_hbm(value):
@@ -299,8 +301,9 @@
         scratch_shapes=[
             pltpu.SMEM((MATS,), jnp.int32),
             pltpu.VMEM((chunks, OWN, MATS, CHUNK), bf16),
-            pltpu.VMEM((OWN * COLS // 128, 128), f32),
-            pltpu.VMEM((COLS // 128, OWN * MATS, 128), f32),
+            pltpu.VMEM((PAD * COLS // 128, 128), f32),
+            pltpu.VMEM((COLS // 128, PAD * MATS, 128), f32),
+            pltpu.VMEM((PAD * COLS // 128, 128), f32),
             pltpu.SemaphoreType.DMA((chunks + 2,)),
         ],
         compiler_params=pltpu.CompilerParams(vmem_limit_bytes=32 * 1024 * 1024),

time: 134 us -> 134 us (level)
  no operation moved by 1% of the time
where the time goes in v7:
time: 134 us; the launch traced here: 133 us
  waiting for transfers between devices  51.8 us (39%)
  blocking collectives  48.3 us (36%)
  Pallas kernels  19.1 us (14%)
  between operations  14.1 us (11%)
    all_gather x1, waiting for transfers between devices, shards(): whole = lax.all_gather(steered, 'fsdp')  51.8 us
    all_to_all x1, blocking collectives, deliver(): lax.all_to_all(pieces, 'rep', split_axis=0, concat_axis=0, tiled=True)  29 us
    all_to_all x1, blocking collectives, deliver(): lax.all_to_all(copies, 'rep', split_axis=0, concat_axis=0, tiled=True, ax...  19.2 us
    pallas_call x1, Pallas kernels, orthogonal_rows(): pl.pallas_call(orthogonal_kernel, out_shape=jax.ShapeDtypeStruct((N_REP,...  14.8 us
  transfers between devices with their start and end apart: 1, of which 1 were waited for; matrix products, arithmetic and copies ran while one was open for 0% of the time, Pallas kernels for 0%

profile of v7, /device:TPU:8, one launch (start us, length us, event | category | flops | bytes accessed | tf_op | source)
XLA Modules:
  0.0 133.3 jit_solution(16430035280656427844)
XLA Ops:
  7.2 0.0 all-gather.3.cloned.1.call-start
  7.2 2.4 %shard_map.50 = (f32[576,128]{1,0:T(8,128)}, f32[576,128]{1,0:T(8,128)}) custom-call(s32[1]{0:T(128)} %bitcast.1.group_ref, s32[8]{0:T(128)} %owners_ref.1, bf16[36,8,2048]{2,1,0:T(8,128)(2,1)} %bitcast.10, f32[576,128]{1,0:T(8,128)} %bitcast.12), custom_call_target="tpu_custom_call" | custom-call | tf_op jit(solution)/shard_map/pallas_call | solution.py:293
  9.6 0.0 all-gather.3.cloned.1.call-update
  9.6 51.8 %all-gather.3.cloned.1.call-done = f32[9216,128]{1,0:T(8,128)} async-done(((f32[576,128]{1,0:T(8,128)}), f32[9216,128]{1,0:T(8,128)}) %all-gather.3.cloned.1.call-update) | async-done | bytes 4718608 | tf_op jit(solution)/shard_map/all_gather | solution.py:326
  61.4 14.8 %shard_map.51 = bf16[32,72,128]{2,1,0:T(8,128)(2,1)S(1)} custom-call(s32[1]{0:T(128)} %bitcast.me_ref, f32[16,576,128]{2,1,0:T(8,128)} %bitcast.9), custom_call_target="tpu_custom_call" | custom-call | tf_op jit(solution)/shard_map/pallas_call | solution.py:177
  76.3 0.0 copy-start
  76.3 29.0 %all_to_all.10.arrived_ref = bf16[32,72,128]{2,1,0:T(8,128)(2,1)S(1)} all-to-all(bf16[32,72,128]{2,1,0:T(8,128)(2,1)S(1)} %shard_map.51), channel_id=1, replica_groups=mesh['rep'=32,'fsdp'=16] {'rep'}, dimensions={0} | all-to-all | bytes 1179648 | tf_op jit(solution)/shard_map/all_to_all | solution.py:314
  105.3 0.0 copy-done
  105.3 0.7 shard_map.52
  106.0 19.2 %all_to_all.11 = bf16[8,576,128]{2,1,0:T(8,128)(2,1)S(1)} all-to-all(bf16[8,576,128]{2,1,0:T(8,128)(2,1)S(1)} %shard_map.52), channel_id=1, replica_groups={{0,16,128,144,256,272,384,400},{32,48,160,176,288,304,416,432},{64,80,1..., dimensions={0} | all-to-all | bytes 2359296 | tf_op jit(solution)/shard_map/all_to_all | solution.py:316
  125.3 1.2 shard_map.53
Async XLA Ops:
  7.2 54.3 %all-gather.3.cloned.1.call-start = ((), (), s32[]{:S(2)}) async-start(), calls=%async_computation.2 | async-start | bytes 5013504 | tf_op jit(solution)/shard_map/all_gather | solution.py:326
  76.3 29.1 %copy-start = (s32[8]{0:T(128)S(1)}, s32[8]{0:T(128)}, u32[]{:S(2)}) copy-start(s32[8]{0:T(128)} %owners_ref.1) | copy-start | bytes 100
Sparse Core Ops, SparseCore 0:
  10.7 50.7 all-gather.2

commit v8 on v7

--- a/solution.py
+++ b/solution.py
@@ -133,7 +133,8 @@
     diagonal = row == col
     total = jnp.sum(jnp.where(diagonal, gram, 0.0), axis=(0, 1), keepdims=True)
     inverse = 1.0 / (jnp.sqrt(total) + EPSILON)
-    g0 = gram * inverse * inverse
+    finite = inverse > 0.0
+    g0 = jnp.where(finite, gram * inverse * inverse, 0.0)
     g0s = split(g0)
     q1s = split(jnp.where(diagonal, QUINTIC_A, 0.0) + QUINTIC_B * g0 + QUINTIC_C * square(g0s))
     g1s = split(symmetric_product(g0s, split(square(q1s))))
@@ -163,6 +164,7 @@
     factor = 0.2 * math.sqrt(max(ROWS, COLS))
     for part in range(chunks):
         update = thin_product(mixed, (high_ref[part], low_ref[part])) * inverse * factor
+        update = jnp.where(finite, update, 0.0)
         for inner in range(CHUNK // WIDE):
             lane = inner * WIDE
             sides = [update[:OWN, lane + side * 128 : lane + (side + 1) * 128] for side in range(SIDES)]

time: 134 us -> 134 us (level)
  no operation moved by 1% of the time
where the time goes in v8:
time: 134 us; the launch traced here: 133 us
  waiting for transfers between devices  51.8 us (39%)
  blocking collectives  48.3 us (36%)
  Pallas kernels  19.1 us (14%)
  between operations  14.1 us (11%)
    all_gather x1, waiting for transfers between devices, shards(): whole = lax.all_gather(steered, 'fsdp')  51.8 us
    all_to_all x1, blocking collectives, deliver(): lax.all_to_all(pieces, 'rep', split_axis=0, concat_axis=0, tiled=True)  29.1 us
    all_to_all x1, blocking collectives, deliver(): lax.all_to_all(copies, 'rep', split_axis=0, concat_axis=0, tiled=True, ax...  19.2 us
    pallas_call x1, Pallas kernels, orthogonal_rows(): pl.pallas_call(orthogonal_kernel, out_shape=jax.ShapeDtypeStruct((N_REP,...  14.9 us
  transfers between devices with their start and end apart: 1, of which 1 were waited for; matrix products, arithmetic and copies ran while one was open for 0% of the time, Pallas kernels for 0%

profile of v8, /device:TPU:8, one launch (start us, length us, event | category | flops | bytes accessed | tf_op | source)
XLA Modules:
  0.0 133.4 jit_solution(17113851042930101860)
XLA Ops:
  7.2 0.0 all-gather.3.cloned.1.call-start
  7.2 2.4 %shard_map.50 = (f32[576,128]{1,0:T(8,128)}, f32[576,128]{1,0:T(8,128)}) custom-call(s32[1]{0:T(128)} %bitcast.1.group_ref, s32[8]{0:T(128)} %owners_ref.1, bf16[36,8,2048]{2,1,0:T(8,128)(2,1)} %bitcast.10, f32[576,128]{1,0:T(8,128)} %bitcast.12), custom_call_target="tpu_custom_call" | custom-call | tf_op jit(solution)/shard_map/pallas_call | solution.py:295
  9.6 0.0 all-gather.3.cloned.1.call-update
  9.6 51.8 %all-gather.3.cloned.1.call-done = f32[9216,128]{1,0:T(8,128)} async-done(((f32[576,128]{1,0:T(8,128)}), f32[9216,128]{1,0:T(8,128)}) %all-gather.3.cloned.1.call-update) | async-done | bytes 4718608 | tf_op jit(solution)/shard_map/all_gather | solution.py:328
  61.4 14.9 %shard_map.51 = bf16[32,72,128]{2,1,0:T(8,128)(2,1)S(1)} custom-call(s32[1]{0:T(128)} %bitcast.me_ref, f32[16,576,128]{2,1,0:T(8,128)} %bitcast.9), custom_call_target="tpu_custom_call" | custom-call | tf_op jit(solution)/shard_map/pallas_call | solution.py:179
  76.3 0.0 copy-start
  76.3 29.1 %all_to_all.10.arrived_ref = bf16[32,72,128]{2,1,0:T(8,128)(2,1)S(1)} all-to-all(bf16[32,72,128]{2,1,0:T(8,128)(2,1)S(1)} %shard_map.51), channel_id=1, replica_groups=mesh['rep'=32,'fsdp'=16] {'rep'}, dimensions={0} | all-to-all | bytes 1179648 | tf_op jit(solution)/shard_map/all_to_all | solution.py:316
  105.4 0.0 copy-done
  105.4 0.7 shard_map.52
  106.1 19.2 %all_to_all.11 = bf16[8,576,128]{2,1,0:T(8,128)(2,1)S(1)} all-to-all(bf16[8,576,128]{2,1,0:T(8,128)(2,1)S(1)} %shard_map.52), channel_id=1, replica_groups={{0,16,128,144,256,272,384,400},{32,48,160,176,288,304,416,432},{64,80,1..., dimensions={0} | all-to-all | bytes 2359296 | tf_op jit(solution)/shard_map/all_to_all | solution.py:318
  125.4 1.2 shard_map.53
Async XLA Ops:
  7.2 54.3 %all-gather.3.cloned.1.call-start = ((), (), s32[]{:S(2)}) async-start(), calls=%async_computation.2 | async-start | bytes 5013504 | tf_op jit(solution)/shard_map/all_gather | solution.py:328
  76.3 29.1 %copy-start = (s32[8]{0:T(128)S(1)}, s32[8]{0:T(128)}, u32[]{:S(2)}) copy-start(s32[8]{0:T(128)} %owners_ref.1) | copy-start | bytes 100
Sparse Core Ops, SparseCore 0:
  10.7 50.7 all-gather.2

commit v9 on v8

--- a/solution.py
+++ b/solution.py
@@ -244,7 +244,48 @@
 
 
 def steer_kernel(
-    group_ref, owners_hbm, grads_hbm, momentum_hbm, renewed_ref, steered_ref,
+    group_ref, owners_hbm, grads_hbm, momentum_hbm, steered_ref,
+    owners_ref, grads_ref, momentum_ref, wide_ref, sems,
+):
+    blocks = COLS // 128
+    chunks = COLS // CHUNK
+
+    def fetch(part):
+        lanes = pl.ds(part * CHUNK, CHUNK)
+        return pltpu.make_async_copy(grads_hbm.at[:, :, lanes], grads_ref.at[part], sems.at[part])
+
+    fetch_owners = pltpu.make_async_copy(owners_hbm, owners_ref, sems.at[chunks])
+    held_rows = pl.ds(0, OWN * blocks)
+    fetch_momentum = pltpu.make_async_copy(momentum_hbm, momentum_ref.at[held_rows], sems.at[chunks + 1])
+    fetch_owners.start()
+    fetch_momentum.start()
+    for part in range(chunks):
+        fetch(part).start()
+    fetch_owners.wait()
+    owns_one = owners_ref[0] == group_ref[0]
+    chosen = 0
+    for index in range(1, MATS):
+        here = owners_ref[index] == group_ref[0]
+        owns_one = jnp.logical_or(owns_one, here)
+        chosen = chosen + jnp.where(here, index, 0)
+    fetch_momentum.wait()
+    for block in range(blocks):
+        part, inner = block // (CHUNK // 128), block % (CHUNK // 128)
+        if inner == 0:
+            fetch(part).wait()
+        wide = grads_ref[part, :, :, inner * 128 : (inner + 1) * 128].astype(f32)
+        wide_ref[block, : OWN * MATS, :] = wide.reshape(OWN * MATS, 128)
+        gradient = wide_ref[block, pl.ds(chosen, PAD, stride=MATS), :]
+        held_state = momentum_ref[pl.ds(block, PAD, stride=blocks), :]
+        renewed = jnp.where(owns_one, MOMENTUM_BETA * held_state + gradient, held_state)
+        steered = gradient + MOMENTUM_BETA * renewed
+        steered_ref[block * STEM : (block + 1) * STEM, :] = steered[:STEM]
+        first = blocks * STEM + block * TAIL
+        steered_ref[first : first + TAIL, :] = steered[STEM:OWN]
+
+
+def renew_kernel(
+    group_ref, owners_hbm, grads_hbm, momentum_hbm, steered_hbm, renewed_ref,
     owners_ref, grads_ref, momentum_ref, wide_ref, fresh_ref, sems,
 ):
     blocks = COLS // 128
@@ -279,10 +320,6 @@
         held_state = momentum_ref[pl.ds(block, PAD, stride=blocks), :]
         renewed = jnp.where(owns_one, MOMENTUM_BETA * held_state + gradient, held_state)
         fresh_ref[pl.ds(block, PAD, stride=blocks), :] = renewed
-        steered = gradient + MOMENTUM_BETA * renewed
-        steered_ref[block * STEM : (block + 1) * STEM, :] = steered[:STEM]
-        first = blocks * STEM + block * TAIL
-        steered_ref[first : first + TAIL, :] = steered[STEM:OWN]
     renewed_ref[...] = fresh_ref[: OWN * blocks, :]
 
 
@@ -290,26 +327,40 @@
     return pltpu.with_memory_space_constraint(value, pltpu.HBM)
 
 
+def read_scratch(*more):
+    chunks = COLS // CHUNK
+    return [
+        pltpu.SMEM((MATS,), jnp.int32),
+        pltpu.VMEM((chunks, OWN, MATS, CHUNK), bf16),
+        pltpu.VMEM((PAD * COLS // 128, 128), f32),
+        pltpu.VMEM((COLS // 128, PAD * MATS, 128), f32),
+        *more,
+        pltpu.SemaphoreType.DMA((chunks + 2,)),
+    ]
+
+
 def steer(owners, group, grads, momentum):
-    chunks = COLS // CHUNK
     return pl.pallas_call(
         steer_kernel,
         in_specs=[pl.BlockSpec(memory_space=pltpu.SMEM)] + [pl.BlockSpec(memory_space=pltpu.HBM)] * 3,
-        out_specs=[pl.BlockSpec(memory_space=pltpu.VMEM)] * 2,
-        out_shape=[
-            jax.ShapeDtypeStruct((OWN * COLS // 128, 128), f32),
-            jax.ShapeDtypeStruct((OWN * COLS // 128, 128), f32),
-        ],
-        scratch_shapes=[
-            pltpu.SMEM((MATS,), jnp.int32),
-            pltpu.VMEM((chunks, OWN, MATS, CHUNK), bf16),
-            pltpu.VMEM((PAD * COLS // 128, 128), f32),
-            pltpu.VMEM((COLS // 128, PAD * MATS, 128), f32),
-            pltpu.VMEM((PAD * COLS // 128, 128), f32),
-            pltpu.SemaphoreType.DMA((chunks + 2,)),
-        ],
+        out_specs=pl.BlockSpec(memory_space=pltpu.VMEM),
+        out_shape=jax.ShapeDtypeStruct((OWN * COLS // 128, 128), f32),
+        scratch_shapes=read_scratch(),
         compiler_params=pltpu.CompilerParams(vmem_limit_bytes=32 * 1024 * 1024),
     )(group, in_hbm(owners), in_hbm(grads), in_hbm(momentum))
+
+
+def renew(owners, group, grads, momentum, steered):
+    return pl.pallas_call(
+        renew_kernel,
+        in_specs=[pl.BlockSpec(memory_space=pltpu.SMEM)]
+        + [pl.BlockSpec(memory_space=pltpu.HBM)] * 3
+        + [pl.BlockSpec(memory_space=pl.ANY)],
+        out_specs=pl.BlockSpec(memory_space=pltpu.VMEM),
+        out_shape=jax.ShapeDtypeStruct((OWN * COLS // 128, 128), f32),
+        scratch_shapes=read_scratch(pltpu.VMEM((PAD * COLS // 128, 128), f32)),
+        compiler_params=pltpu.CompilerParams(vmem_limit_bytes=32 * 1024 * 1024),
+    )(group, in_hbm(owners), in_hbm(grads), in_hbm(momentum), steered)
 
 
 def deliver(pieces, owners):
@@ -324,7 +375,9 @@
     group = lax.axis_index("rep").astype(jnp.int32)[None]
     position = lax.axis_index("fsdp").astype(jnp.int32)[None]
     flat = momentum.reshape(OWN * COLS // 128, 128)
-    renewed, steered = steer(owners, group, grads.transpose(1, 0, 2), flat)
+    by_row = grads.transpose(1, 0, 2)
+    steered = steer(owners, group, by_row, flat)
+    renewed = renew(owners, group, by_row, flat, steered)
     whole = lax.all_gather(steered, "fsdp")
     pieces = orthogonal_rows(position, in_hbm(whole))
     update = deliver(pieces, owners)

time: 134 us -> 134 us (level)
  blocking collectives: 48.3 us -> 29.1 us
  waiting for transfers between devices: 51.8 us -> 64.3 us
  starting transfers between devices: 0.04 us -> 4.33 us
  Pallas kernels: 19.1 us -> 22.2 us
    all_to_all x1 -> x0, blocking collectives: 19.2 us -> none  [deliver(): lax.all_to_all(copies, 'rep', split_axis=0, concat_axis=0, tiled=True, ax...]
    all_to_all x0 -> x1, waiting for transfers between devices: none -> 12.9 us  [deliver(): lax.all_to_all(copies, 'rep', split_axis=0, concat_axis=0, tiled=True, ax...]
    all_to_all x0 -> x1, starting transfers between devices: none -> 4.29 us  [deliver(): lax.all_to_all(copies, 'rep', split_axis=0, concat_axis=0, tiled=True, ax...]
    pallas_call x0 -> x1, Pallas kernels: none -> 2.24 us  [renew(): pl.pallas_call(renew_kernel, in_specs=[pl.BlockSpec(memory_space=pltpu.SM...]
  transfers between devices with their start and end apart: 1 -> 2, of which waited for: 1 -> 2; matrix products, arithmetic and copies ran while one was open for 0% -> 0% of each run, Pallas kernels for 0% -> 2%
where the time goes in v9:
time: 134 us
  waiting for transfers between devices  64.3 us (48%)
  blocking collectives  29.1 us (22%)
  Pallas kernels  22.2 us (17%)
  between operations  14.1 us (11%)
  starting transfers between devices  4.33 us (3%)
    all_gather x1, waiting for transfers between devices, shards(): whole = lax.all_gather(steered, 'fsdp')  51.4 us
    all_to_all x1, blocking collectives, deliver(): lax.all_to_all(pieces, 'rep', split_axis=0, concat_axis=0, tiled=True)  29.1 us
    pallas_call x1, Pallas kernels, orthogonal_rows(): pl.pallas_call(orthogonal_kernel, out_shape=jax.ShapeDtypeStruct((N_REP,...  14.9 us
    all_to_all x1, waiting for transfers between devices, deliver(): lax.all_to_all(copies, 'rep', split_axis=0, concat_axis=0, tiled=True, ax...  12.9 us
    all_to_all x1, starting transfers between devices, deliver(): lax.all_to_all(copies, 'rep', split_axis=0, concat_axis=0, tiled=True, ax...  4.29 us
  transfers between devices with their start and end apart: 2, of which 2 were waited for; matrix products, arithmetic and copies ran while one was open for 0% of the time, Pallas kernels for 2%

profile of v9, /device:TPU:8, one launch (start us, length us, event | category | flops | bytes accessed | tf_op | source)
XLA Modules:
  0.0 134.0 jit_solution(13090999241167738214)
XLA Ops:
  7.2 0.0 all-gather.3.cloned.1.call-start
  7.2 2.2 %shard_map.50.steered_hbm = f32[576,128]{1,0:T(8,128)} custom-call(s32[1]{0:T(128)} %bitcast.1.group_ref, s32[8]{0:T(128)} %owners_hbm.3, bf16[36,8,2048]{2,1,0:T(8,128)(2,1)} %bitcast.9, f32[576,128]{1,0:T(8,128)} %bitcast.12), custom_call_target="tpu_custom_call" | custom-call | tf_op jit(solution)/shard_map/pallas_call | solution.py:343
  9.4 0.0 all-gather.3.cloned.1.call-update
  9.4 51.4 %all-gather.3.cloned.1.call-done = f32[9216,128]{1,0:T(8,128)} async-done(((f32[576,128]{1,0:T(8,128)}), f32[9216,128]{1,0:T(8,128)}) %all-gather.3.cloned.1.call-update) | async-done | bytes 4718608 | tf_op jit(solution)/shard_map/all_gather | solution.py:381
  60.9 14.9 %shard_map.51 = bf16[32,72,128]{2,1,0:T(8,128)(2,1)S(1)} custom-call(s32[1]{0:T(128)} %bitcast.me_ref, f32[16,576,128]{2,1,0:T(8,128)} %bitcast.11), custom_call_target="tpu_custom_call" | custom-call | tf_op jit(solution)/shard_map/pallas_call | solution.py:179
  75.7 0.0 copy-start
  75.8 29.1 %all_to_all.10.arrived_ref = bf16[32,72,128]{2,1,0:T(8,128)(2,1)S(1)} all-to-all(bf16[32,72,128]{2,1,0:T(8,128)(2,1)S(1)} %shard_map.51), channel_id=1, replica_groups=mesh['rep'=32,'fsdp'=16] {'rep'}, dimensions={0} | all-to-all | bytes 1179648 | tf_op jit(solution)/shard_map/all_to_all | solution.py:367
  104.8 0.0 copy-done
  104.8 1.7 %shard_map.52 = bf16[8,576,128]{2,1,0:T(8,128)(2,1)} custom-call(s32[8]{0:T(128)S(1)} %copy-done, bf16[32,72,128]{2,1,0:T(8,128)(2,1)S(1)} %all_to_all.10.arrived_ref), custom_call_target="tpu_custom_call" | custom-call | tf_op jit(solution)/shard_map/pallas_call | solution.py:207
  106.5 4.3 %all-to-all-start.1 = ((bf16[8,576,128]{2,1,0:T(8,128)(2,1)}), bf16[8,576,128]{2,1,0:T(8,128)(2,1)S(1)}, u32[]{:S(2)}, u32[]{:S(2)}) async-start(bf16[8,576,128]{2,1,0:T(8,128)(2,1)} %shard_map.52), calls=%async_computation.1 | async-start | bytes 2359296 | tf_op jit(solution)/shard_map/all_to_all | solution.py:369
  110.8 2.2 %shard_map.54 = f32[576,128]{1,0:T(8,128)} custom-call(s32[1]{0:T(128)} %bitcast.1.group_ref, s32[8]{0:T(128)} %owners_hbm.3, bf16[36,8,2048]{2,1,0:T(8,128)(2,1)} %bitcast.10, f32[576,128]{1,0:T(8,128)} %bitcast.13, f32[576,128]{1,0:T(8,128)} %shard_map.50.steered_hbm), custom_call_target="tpu_custom_call" | custom-call | tf_op jit(solution)/shard_map/pallas_call | solution.py:354
  113.1 12.9 %all-to-all-done.1 = bf16[8,576,128]{2,1,0:T(8,128)(2,1)S(1)} async-done(((bf16[8,576,128]{2,1,0:T(8,128)(2,1)}), bf16[8,576,128]{2,1,0:T(8,128)(2,1)S(1)}, u32[]{:S(2)}, u32[]{:S(2)}) %all-to-all-start.1) | async-done | bytes 1179680 | tf_op jit(solution)/shard_map/all_to_all | solution.py:369
  126.0 1.2 shard_map.53
Async XLA Ops:
  7.2 53.7 %all-gather.3.cloned.1.call-start = ((), (), s32[]{:S(2)}) async-start(), calls=%async_computation.2 | async-start | bytes 5013504 | tf_op jit(solution)/shard_map/all_gather | solution.py:381
  75.7 29.1 %copy-start = (s32[8]{0:T(128)S(1)}, s32[8]{0:T(128)}, u32[]{:S(2)}) copy-start(s32[8]{0:T(128)} %owners_hbm.3) | copy-start | bytes 100
  106.5 19.4 %all-to-all-start.1 = ((bf16[8,576,128]{2,1,0:T(8,128)(2,1)}), bf16[8,576,128]{2,1,0:T(8,128)(2,1)S(1)}, u32[]{:S(2)}, u32[]{:S(2)}) async-start(bf16[8,576,128]{2,1,0:T(8,128)(2,1)} %shard_map.52), calls=%async_computation.1 | async-start | bytes 2359296 | tf_op jit(solution)/shard_map/all_to_all | solution.py:369
Sparse Core Ops, SparseCore 0:
  10.1 50.7 all-gather.2

commit v10 on v9

--- a/solution.py
+++ b/solution.py
@@ -96,7 +96,7 @@
     return first[:PAD] + (first[PAD:] + second)
 
 
-def orthogonal_kernel(me_ref, s_hbm, u_ref, stem_ref, tail_ref, high_ref, low_ref, sems):
+def orthogonal_kernel(me_ref, s_hbm, renewed_hbm, u_ref, stem_ref, tail_ref, high_ref, low_ref, sems):
     chunks = COLS // CHUNK
     blocks = CHUNK // 128
 
@@ -174,7 +174,7 @@
                     u_ref[group] = piece
 
 
-def orthogonal_rows(position, whole):
+def orthogonal_rows(position, whole, renewed):
     chunks = COLS // CHUNK
     return pl.pallas_call(
         orthogonal_kernel,
@@ -182,6 +182,7 @@
         in_specs=[
             pl.BlockSpec(memory_space=pltpu.SMEM),
             pl.BlockSpec(memory_space=pltpu.HBM),
+            pl.BlockSpec(memory_space=pl.ANY),
         ],
         out_specs=pl.BlockSpec(memory_space=pltpu.VMEM),
         scratch_shapes=[
@@ -192,7 +193,7 @@
             pltpu.SemaphoreType.DMA((chunks + 1,)),
         ],
         compiler_params=pltpu.CompilerParams(vmem_limit_bytes=48 * 1024 * 1024),
-    )(position, whole)
+    )(position, whole, renewed)
 
 
 def choose_kernel(owners_ref, arrived_ref, out_ref, rows_ref):
@@ -379,7 +380,7 @@
     steered = steer(owners, group, by_row, flat)
     renewed = renew(owners, group, by_row, flat, steered)
     whole = lax.all_gather(steered, "fsdp")
-    pieces = orthogonal_rows(position, in_hbm(whole))
+    pieces = orthogonal_rows(position, in_hbm(whole), renewed)
     update = deliver(pieces, owners)
     return (update, renewed.reshape(1, OWN, COLS))
 

time: 134 us -> 135 us (level)
  blocking collectives: 29.1 us -> 48.3 us
  waiting for transfers between devices: 64.3 us -> 49.8 us
  starting transfers between devices: 4.33 us -> 0.04 us
    all_to_all x0 -> x1, blocking collectives: none -> 19.2 us  [deliver(): lax.all_to_all(copies, 'rep', split_axis=0, concat_axis=0, tiled=True, ax...]
    all_to_all x1 -> x0, waiting for transfers between devices: 12.9 us -> none  [deliver(): lax.all_to_all(copies, 'rep', split_axis=0, concat_axis=0, tiled=True, ax...]
    all_to_all x1 -> x0, starting transfers between devices: 4.29 us -> none  [deliver(): lax.all_to_all(copies, 'rep', split_axis=0, concat_axis=0, tiled=True, ax...]
    all_gather x1, waiting for transfers between devices: 51.4 us -> 49.8 us  [shards(): whole = lax.all_gather(steered, 'fsdp')]
  transfers between devices with their start and end apart: 2 -> 1, of which waited for: 2 -> 1; matrix products, arithmetic and copies ran while one was open for 0% -> 0% of each run, Pallas kernels for 2% -> 2%
where the time goes in v10:
time: 135 us; the launch traced here: 134 us
  waiting for transfers between devices  49.8 us (37%)
  blocking collectives  48.3 us (36%)
  Pallas kernels  21.2 us (16%)
  between operations  14.1 us (10%)
    all_gather x1, waiting for transfers between devices, shards(): whole = lax.all_gather(steered, 'fsdp')  49.8 us
    all_to_all x1, blocking collectives, deliver(): lax.all_to_all(pieces, 'rep', split_axis=0, concat_axis=0, tiled=True)  29 us
    all_to_all x1, blocking collectives, deliver(): lax.all_to_all(copies, 'rep', split_axis=0, concat_axis=0, tiled=True, ax...  19.2 us
    pallas_call x1, Pallas kernels, orthogonal_rows(): pl.pallas_call(orthogonal_kernel, out_shape=jax.ShapeDtypeStruct((N_REP,...  14.9 us
  transfers between devices with their start and end apart: 1, of which 1 were waited for; matrix products, arithmetic and copies ran while one was open for 0% of the time, Pallas kernels for 2%

profile of v10, /device:TPU:8, one launch (start us, length us, event | category | flops | bytes accessed | tf_op | source)
XLA Modules:
  0.0 134.4 jit_solution(10582107190739208752)
XLA Ops:
  7.2 0.0 all-gather.3.cloned.1.call-start
  7.2 2.2 %shard_map.50.steered_hbm = f32[576,128]{1,0:T(8,128)} custom-call(s32[1]{0:T(128)} %bitcast.1.group_ref, s32[8]{0:T(128)} %owners_ref.1, bf16[36,8,2048]{2,1,0:T(8,128)(2,1)} %bitcast.10, f32[576,128]{1,0:T(8,128)} %bitcast.13), custom_call_target="tpu_custom_call" | custom-call | tf_op jit(solution)/shard_map/pallas_call | solution.py:344
  9.4 0.0 all-gather.3.cloned.1.call-update
  9.4 2.2 %shard_map.51.renewed_hbm = f32[576,128]{1,0:T(8,128)} custom-call(s32[1]{0:T(128)} %bitcast.1.group_ref, s32[8]{0:T(128)} %owners_ref.1, bf16[36,8,2048]{2,1,0:T(8,128)(2,1)} %bitcast.11, f32[576,128]{1,0:T(8,128)} %bitcast.14, f32[576,128]{1,0:T(8,128)} %shard_map.50.steered_hbm), custom_call_target="tpu_custom_call" | custom-call | tf_op jit(solution)/shard_map/pallas_call | solution.py:355
  11.7 49.8 %all-gather.3.cloned.1.call-done = f32[9216,128]{1,0:T(8,128)} async-done(((f32[576,128]{1,0:T(8,128)}), f32[9216,128]{1,0:T(8,128)}) %all-gather.3.cloned.1.call-update) | async-done | bytes 4718608 | tf_op jit(solution)/shard_map/all_gather | solution.py:382
  61.4 0.0 copy-start
  61.5 1.0 copy-done
  62.4 14.9 %shard_map.52 = bf16[32,72,128]{2,1,0:T(8,128)(2,1)S(1)} custom-call(s32[1]{0:T(128)} %bitcast.me_ref, f32[16,576,128]{2,1,0:T(8,128)} %bitcast.12, f32[576,128]{1,0:T(8,128)S(1)} %copy-done), custom_call_target="tpu_custom_call" | custom-call | tf_op jit(solution)/shard_map/pallas_call | solution.py:179
  77.3 0.0 copy-start.1
  77.3 29.0 %all_to_all.10.arrived_ref = bf16[32,72,128]{2,1,0:T(8,128)(2,1)S(1)} all-to-all(bf16[32,72,128]{2,1,0:T(8,128)(2,1)S(1)} %shard_map.52), channel_id=1, replica_groups=mesh['rep'=32,'fsdp'=16] {'rep'}, dimensions={0} | all-to-all | bytes 1179648 | tf_op jit(solution)/shard_map/all_to_all | solution.py:368
  106.4 0.0 copy-done.1
  106.4 0.7 shard_map.53
  107.1 19.2 %all_to_all.11 = bf16[8,576,128]{2,1,0:T(8,128)(2,1)S(1)} all-to-all(bf16[8,576,128]{2,1,0:T(8,128)(2,1)S(1)} %shard_map.53), channel_id=1, replica_groups={{0,16,128,144,256,272,384,400},{32,48,160,176,288,304,416,432},{64,80,1..., dimensions={0} | all-to-all | bytes 2359296 | tf_op jit(solution)/shard_map/all_to_all | solution.py:370
  126.3 1.2 shard_map.54
Async XLA Ops:
  7.2 54.3 %all-gather.3.cloned.1.call-start = ((), (), s32[]{:S(2)}) async-start(), calls=%async_computation.2 | async-start | bytes 5013504 | tf_op jit(solution)/shard_map/all_gather | solution.py:382
  61.4 1.0 copy-start
  77.3 29.1 %copy-start.1 = (s32[8]{0:T(128)S(1)}, s32[8]{0:T(128)}, u32[]{:S(2)}) copy-start(s32[8]{0:T(128)} %owners_ref.1) | copy-start | bytes 100
Sparse Core Ops, SparseCore 0:
  10.7 50.7 all-gather.2
